TPU v7x, 128 devices: a whole 4x4x4 slice. The times are simulated.
128 devices in a mesh: grp: 2 (over core), shard: 64 (over z, y, x).
Axes of the slice: x: 4, y: 4, z: 4, core: 2. Of those that a mesh axis runs over, the one named last changes fastest.
Arguments:
- tokens: bfloat16 [32768, 1536], P(('grp', 'shard')), may hold values from -6 to 6
- segment_ids: int32 [128, 256], P(('grp', 'shard')), may hold values from 0 to 7, never falling along the last dimension, each value on 1 to 128 neighbouring positions
- norm_gain: float32 [1536], replicated, may hold values from 0.5 to 1.5
- in_weight: bfloat16 [1536, 6448], P('shard'), may hold values from -0.15625 to 0.15625
- conv_weight: float32 [4, 3328], replicated, may hold values from -3 to 3
- conv_bias: float32 [3328], replicated, may hold values from -2 to 2
- dt_bias: float32 [48], replicated, may hold values from -5 to -2
- a_log: float32 [48], replicated, may hold values from -0.5 to 2.5
- skip_d: float32 [48], replicated, may hold values from 0.5 to 1.5
- gnorm_gain: float32 [3072], replicated, may hold values from 0.5 to 1.5
- out_weight: bfloat16 [3072, 1536], P('shard'), may hold values from -0.109375 to 0.109375
- cotangent: bfloat16 [32768, 1536], P(('grp', 'shard')), may hold values from -6 to 6
Outputs:
- out_tokens: bfloat16 [32768, 1536], P(('grp', 'shard'))
- grad_tokens: float32 [32768, 1536], P(('grp', 'shard'))
- grad_norm_gain: float32 [1536], replicated
- grad_in_weight: float32 [1536, 6448], P('shard')
- grad_conv_weight: float32 [4, 3328], replicated
- grad_conv_bias: float32 [3328], replicated
- grad_dt_bias: float32 [48], replicated
- grad_a_log: float32 [48], replicated
- grad_skip_d: float32 [48], replicated
- grad_gnorm_gain: float32 [3072], replicated
- grad_out_weight: float32 [3072, 1536], P('shard')
Inputs may be any that keep to these rules, and one draw needn't show every extreme that they name: `segment_ids`: segment ids never fall along a sequence; each document holds at most 128 tokens and one holds exactly that many.
All inputs are finite; a program needn't handle non-finite values.
Results may differ from a plain program's by a relative error of at most 0.0073.
Values may be sent and summed in bfloat16 or wider, within the bound.
No kernel may reach another device: no remote copies, remote signals or barrier semaphores. Data moves between devices by JAX's collectives and lax.ppermute only.
A program may use at most 256 MiB of HBM per device.

v0:
```python
import jax
import jax.numpy as jnp
from jax import lax
from jax.sharding import PartitionSpec as P

SPAN = 256


norm_eps = 1e-05
highest = lax.Precision.HIGHEST


def sent_to_all(shard, axis):
    copies = jnp.broadcast_to(shard, (lax.axis_size(axis), *shard.shape))
    return lax.all_to_all(copies, axis, split_axis=0, concat_axis=0, tiled=True)


def of_everyone(shard, axis):
    return sent_to_all(shard, axis).sum(axis=0)


def in_one(arrays, axis):
    flat, at, outs = (jnp.concatenate([a.reshape(-1) for a in arrays]), 0, [])
    total = of_everyone(flat, axis)
    for a in arrays:
        outs.append(total[at : at + a.size].reshape(a.shape))
        at += a.size
    return tuple(outs)


def rms_gain(values, gain):
    return values * lax.rsqrt(jnp.mean(values * values, axis=-1, keepdims=True) + norm_eps) * gain


def block_step(carry, pieces):
    ssm_state, prev_doc = carry
    x_block, b_block, c_block, dt_block, rate_block, seg_block = pieces
    cumulative = jnp.cumsum(rate_block, axis=0)
    position = jnp.arange(seg_block.shape[0])
    causal_same = (
        (position[:, None] >= position[None, :]) & (seg_block[:, None] == seg_block[None, :])
    ).astype(rate_block.dtype)
    log_gap = cumulative[:, None, :] - cumulative[None, :, :]
    decay_table = (
        jnp.exp(jnp.where(causal_same[:, :, None] > 0, log_gap, 0.0)) * causal_same[:, :, None]
    )
    scores = jnp.dot(c_block, b_block.T, precision=highest)
    weights = scores[:, :, None] * decay_table * dt_block[None, :, :]
    inside = jnp.einsum("tsh,shp->thp", weights, x_block, precision=highest)
    keep_state = (seg_block == prev_doc).astype(rate_block.dtype)
    from_state = (
        jnp.einsum("tn,hpn->thp", c_block, ssm_state, precision=highest)
        * (keep_state[:, None] * jnp.exp(cumulative))[:, :, None]
    )
    last_doc = seg_block[-1]
    tail_weight = (
        jnp.exp(cumulative[-1][None, :] - cumulative)
        * dt_block
        * (seg_block == last_doc).astype(rate_block.dtype)[:, None]
    )
    carried = (
        (last_doc == prev_doc).astype(rate_block.dtype)
        * jnp.exp(cumulative[-1])[:, None, None]
        * ssm_state
    )
    state_new = carried + jnp.einsum(
        "sh,shp,sn->hpn", tail_weight, x_block, b_block, precision=highest
    )
    return ((state_new, last_doc), inside + from_state)


def mix_layer(projected, segments, conv_weight, conv_bias, dt_bias, a_log, skip_d, gnorm_gain):
    length = projected.shape[0]
    inner_width = gnorm_gain.shape[0]
    head_count = dt_bias.shape[0]
    head_dim = inner_width // head_count
    conv_width = conv_bias.shape[0]
    state_dim = (conv_width - inner_width) // 2
    tap_count = conv_weight.shape[0]
    gate_part = projected[:, :inner_width]
    conv_input = projected[:, inner_width : inner_width + conv_width]
    dt_raw = projected[:, inner_width + conv_width :]
    seg_padded = jnp.concatenate([jnp.full((tap_count - 1,), -1, jnp.int32), segments])
    input_padded = jnp.concatenate(
        [jnp.zeros((tap_count - 1, conv_width), projected.dtype), conv_input], axis=0
    )
    convolved = conv_bias + jnp.zeros_like(conv_input)
    for tap_index in range(tap_count):
        shifted = input_padded[tap_index : tap_index + length]
        same_doc = (seg_padded[tap_index : tap_index + length] == segments).astype(projected.dtype)
        convolved = convolved + conv_weight[tap_index] * shifted * same_doc[:, None]
    activated = jax.nn.silu(convolved)
    x_heads = activated[:, :inner_width].reshape(length, head_count, head_dim)
    b_matrix = activated[:, inner_width : inner_width + state_dim]
    c_matrix = activated[:, inner_width + state_dim :]
    step_size = jax.nn.softplus(dt_raw + dt_bias)
    log_decay = -step_size * jnp.exp(a_log)
    block_count = length // SPAN
    pieces = (
        x_heads.reshape(block_count, SPAN, head_count, head_dim),
        b_matrix.reshape(block_count, SPAN, state_dim),
        c_matrix.reshape(block_count, SPAN, state_dim),
        step_size.reshape(block_count, SPAN, head_count),
        log_decay.reshape(block_count, SPAN, head_count),
        segments.reshape(block_count, SPAN),
    )
    start_carry = (
        jnp.zeros((head_count, head_dim, state_dim), projected.dtype),
        jnp.array(-1, jnp.int32),
    )
    ignored, block_out = lax.scan(jax.checkpoint(block_step), start_carry, pieces)
    mixed_out = block_out.reshape(length, head_count, head_dim) + skip_d[:, None] * x_heads
    gated_out = mixed_out.reshape(length, inner_width) * jax.nn.silu(gate_part)
    return rms_gain(gated_out, gnorm_gain)


def times_rows(left, piece):
    return lax.dot_general(
        left, piece, (((1,), (1,)), ((), ())), preferred_element_type=jnp.float32
    )


def on_device(
    tokens,
    segment_ids,
    norm_gain,
    in_weight,
    conv_weight,
    conv_bias,
    dt_bias,
    a_log,
    skip_d,
    gnorm_gain,
    out_weight,
    cotangent,
):
    residual_in = tokens.astype(jnp.float32)
    normed, norm_back = jax.vjp(rms_gain, residual_in, norm_gain)
    normed_low = normed.astype(jnp.bfloat16)
    segments = segment_ids[0]

    def add_rows(left, piece):
        return jnp.dot(left, piece, preferred_element_type=jnp.float32)

    projected = add_rows(normed_low, lax.all_gather(in_weight, "shard", axis=0, tiled=True))

    def local_mixer(proj_part, conv_taps, conv_shift, dt_shift, decay_log, skip_head, gain_gated):
        return mix_layer(
            proj_part, segments, conv_taps, conv_shift, dt_shift, decay_log, skip_head, gain_gated
        )

    mixer_out, mixer_back = jax.vjp(
        local_mixer, projected, conv_weight, conv_bias, dt_bias, a_log, skip_d, gnorm_gain
    )
    mixer_low = mixer_out.astype(jnp.bfloat16)
    branch_out = add_rows(mixer_low, lax.all_gather(out_weight, "shard", axis=0, tiled=True))
    out_tokens = (residual_in + branch_out).astype(jnp.bfloat16)
    local_out_grad = lax.dot_general(
        mixer_low, cotangent, (((0,), (0,)), ((), ())), preferred_element_type=jnp.float32
    )
    grad_mixer = times_rows(cotangent, lax.all_gather(out_weight, "shard", axis=0, tiled=True))
    grad_proj, grad_taps, grad_shift, grad_dt, grad_decay, grad_skip, grad_gated = mixer_back(
        grad_mixer
    )
    grad_proj_low = grad_proj.astype(jnp.bfloat16)
    local_in_grad = lax.dot_general(
        normed_low, grad_proj_low, (((0,), (0,)), ((), ())), preferred_element_type=jnp.float32
    )
    grad_normed = times_rows(grad_proj_low, lax.all_gather(in_weight, "shard", axis=0, tiled=True))
    grad_from_norm, grad_gain = norm_back(grad_normed)
    grad_tokens = cotangent.astype(jnp.float32) + grad_from_norm
    share_in, share_out = (
        lax.psum_scatter(local_in_grad, "shard", scatter_dimension=0, tiled=True),
        lax.psum_scatter(local_out_grad, "shard", scatter_dimension=0, tiled=True),
    )
    grad_in_weight, grad_out_weight = in_one((share_in, share_out), "grp")
    summed = lax.psum(
        (grad_gain, grad_taps, grad_shift, grad_dt, grad_decay, grad_skip, grad_gated),
        ("grp", "shard"),
    )
    return (
        out_tokens,
        grad_tokens,
        summed[0],
        grad_in_weight,
        summed[1],
        summed[2],
        summed[3],
        summed[4],
        summed[5],
        summed[6],
        grad_out_weight,
    )


def solution(mesh):
    return jax.shard_map(
        on_device,
        mesh=mesh,
        in_specs=(
            P(("grp", "shard"), None),
            P(("grp", "shard"), None),
            P(),
            P("shard", None),
            P(),
            P(),
            P(),
            P(),
            P(),
            P(),
            P("shard", None),
            P(("grp", "shard"), None),
        ),
        out_specs=(
            P(("grp", "shard"), None),
            P(("grp", "shard"), None),
            P(),
            P("shard", None),
            P(),
            P(),
            P(),
            P(),
            P(),
            P(),
            P("shard", None),
        ),
        check_vma=False,
    )
```

profile of v0, /device:TPU:1, one launch (start us, length us, event | category | flops | bytes accessed | tf_op | source)
XLA Modules:
  0.0 896.1 jit_solution(1493276473429490417)
XLA Ops:
  11.8 1.4 fusion.54
  13.2 1.4 compare_convert_fusion.2
  14.6 1.6 broadcast_compare_fusion.1
  16.2 112.0 %all-gather.3.cloned.1.call-done = bf16[1536,6448]{1,0:T(8,128)(2,1)} async-done(((bf16[24,6448]{1,0:T(8,128)(2,1)}), bf16[1536,6448]{1,0:T(8,128)(2,1)}) %all-gather.3.cloned.1.call-update) | async-done | bytes 19808272 | tf_op jit(solution)/shard_map/all_gather | solution.py:145
  128.2 9.9 %fusion.74 = f32[256,6448]{1,0:T(8,128)S(1)} fusion(bf16[1536,6448]{1,0:T(8,128)(2,1)} %all-gather.3.cloned.1.call-done, bf16[256,1536]{1,0:T(8,128)(2,1)} %param.12, f32[1536]{0:T(1024)} %param.14, f32[256]{0:T(256)S(1)} %fusion.86), kind=kOutput, calls=%fused_computation.112 | convolution fusion | flops 5072486400 | bytes 27204608 | tf_op jit(solution)/shard_map/dot_general | solution.py:143
  138.4 2.5 copy-done.9
  141.0 4.1 fusion.31
  145.1 2.0 slice.113
  147.1 3.6 copy.153
  150.7 1.7 negate_multiply_fusion
  153.1 1.6 copy.155
  154.7 1.9 reduce-window.20
  156.6 1.5 slice_reduce_fusion.2
  161.2 2.6 fusion.66
  163.9 15.7 %bitcast_add_fusion.1 = f32[256,48,64]{0,2,1:T(8,128)} fusion(f32[256,48,64]{0,2,1:T(8,128)S(1)} %fusion.66, f32[256,48,64]{0,2,1:T(8,128)S(1)} %bitcast.126, f32[256,48]{0,1:T(8,128)S(1)} %copy-done.35, f32[256,256]{1,0:T(8,128)S(1)} %copy-done.16, f32[256,48]{0,1:T(8,128)S(1)} %bitcast_bitcast_fusion, f32[256,256]{1,0:T(8,128)S(1)} %fusion.92, ...), kind=kOutput, calls=%fused_computation.60 | convolution fusion | flops 2433220608 | bytes 10174464 | tf_op jit(solution)/shard_map/jvp()/while/body/eval_jaxpr/tsh,shp->thp/dot_general | solution.py:49
  179.6 3.9 copy.158
  183.5 4.1 multiply_reduce_fusion.10
  189.3 8.3 fusion.97
  197.6 14.6 %all-gather.5.cloned.1.call-done = bf16[3072,1536]{1,0:T(8,128)(2,1)} async-done(((bf16[48,1536]{1,0:T(8,128)(2,1)}), bf16[3072,1536]{1,0:T(8,128)(2,1)}) %all-gather.5.cloned.1.call-update) | async-done | bytes 9437200 | tf_op jit(solution)/shard_map/all_gather | solution.py:156
  212.2 8.4 multiply_reduce_fusion.6
  221.3 6.3 multiply_reduce_fusion.7
  227.6 3.6 copy.160
  234.8 1.4 fusion.104
  236.3 22.4 %fusion.14 = (f32[256,48]{0,1:T(8,128)S(1)}, f32[256,48]{0,1:T(8,128)S(1)}, f32[256,48]{0,1:T(8,128)}, f32[256,256]{1,0:T(8,128)S(1)}) fusion(f32[256,48]{0,1:T(8,128)S(1)} %copy.167, f32[256,256]{1,0:T(8,128)S(1)} %get-tuple-element.172, f32[256,48]{0,1:T(8,128)S(1)} %copy.163, f32[256,256]{1,0:T(8,128)S(1)} %fusion.104, ...), kind=kOutput, calls=%fused_computation.19 | convolution fusion | flops 2463002624 | bytes 7389184 | tf_op jit(solution)/shard_map/transpose(jvp())/while/body/eval_jaxpr/checkpoint/tsh,shp->thp/dot_general | solution.py:49
  259.1 4.3 multiply_reduce_fusion.8
  264.1 5.7 multiply_reduce_fusion.5
  271.4 14.1 %bitcast_add_fusion = f32[256,48,64]{0,2,1:T(8,128)} fusion(f32[256,48,64]{0,2,1:T(8,128)} %get-tuple-element.181, f32[256,48]{0,1:T(8,128)} %copy-done.33, f32[256,256]{1,0:T(8,128)S(1)} %get-tuple-element.172, f32[256,48]{0,1:T(8,128)} %copy-done.34, f32[256,256]{1,0:T(8,128)} %copy-done.17, pred[256,256]{1,0:T(8,128)(4,1)} %copy-done.30, ...), kind=kOutput, calls=%fused_computation.56 | convolution fusion | flops 2433220608 | bytes 10174464 | tf_op jit(solution)/shard_map/transpose(jvp())/while/body/eval_jaxpr/checkpoint/tsh,shp->thp/dot_general | solution.py:49
  285.5 3.7 copy.174
  289.3 2.7 reduce-window.26
  292.5 7.2 fusion.63
  300.3 5.1 fusion.60
  305.8 2.2 fusion.99
  308.6 1.5 copy-done.1
  311.2 6.3 multiply_reduce_fusion.3
  319.8 18.6 %fusion.72 = f32[1536,6448]{1,0:T(8,128)} fusion(bf16[256,1536]{1,0:T(8,128)(2,1)} %param.12, f32[1536]{0:T(1024)S(1)} %copy-done.18, f32[256]{0:T(256)S(1)} %copy-done.38, f32[256,3072]{1,0:T(8,128)} %get-tuple-element.156, f32[256,3328]{1,0:T(8,128)S(1)} %pad_add_fusion, f32[256,48]{1,0:T(8,128)S(1)} %copy-done.15), kind=kOutput, calls=%fused_computation.111 | convolution fusion | flops 5077438464 | bytes 47012864 | tf_op jit(solution)/shard_map/dot_general | solution.py:166
  343.8 1.4 reduce_sum.280
  347.7 12.4 %fusion.52 = (f32[1536]{0:T(1024)}, f32[256]{0:T(256)}, f32[256,1536]{1,0:T(8,128)}) fusion(bf16[256,1536]{1,0:T(8,128)(2,1)} %param.12, f32[256]{0:T(256)S(1)} %copy-done.38, f32[1536]{0:T(1024)S(1)} %copy-done.18, bf16[1536,6448]{1,0:T(8,128)(2,1)} %all-gather.3.cloned.1.call-done, f32[256,3072]{1,0:T(8,128)} %get-tuple-element.156, ...), kind=kOutput, calls=%fused_computation.87 | convolution fusion | flops 5078616064 | bytes 28784640 | tf_op jit(solution)/shard_map/dot_general | solution.py:118
  361.0 1.6 pad_add_fusion.3
  362.6 3.5 fusion.53
  366.1 7.5 fusion.42
  373.6 80.0 %reduce-scatter.5.cloned.1.call-done = f32[48,1536]{1,0:T(8,128)} async-done(((f32[3072,1536]{1,0:T(8,128)}), f32[48,1536]{1,0:T(8,128)}) %reduce-scatter.5.cloned.1.call-update) | async-done | bytes 294928 | tf_op jit(solution)/shard_map/reduce_scatter | solution.py:174
  454.6 277.9 %reduce-scatter.7.cloned.1.call-done = f32[24,6448]{1,0:T(8,128)} async-done(((f32[1536,6448]{1,0:T(8,128)}), f32[24,6448]{1,0:T(8,128)}) %reduce-scatter.7.cloned.1.call-update) | async-done | bytes 619024
  732.5 1.5 reshape.430
  734.1 4.3 broadcast_in_dim.138
  738.4 7.0 all_to_all.6
  745.4 8.5 reduce_sum.265
  756.0 124.4 %all-reduce.22.cloned.1.call-done = (f32[1536]{0:T(1024)}, f32[4,3328]{1,0:T(4,128)}, f32[3328]{0:T(1024)}, f32[48]{0:T(128)}, f32[48]{0:T(128)}, /*index=5*/f32[48]{0:T(128)}, f32[3072]{0:T(1024)}) async-done(((f32[1536]{0:T(1024)}, f32[4,3328]{1,0:T(4,128)}, f32[3328]{0:T(1024)}, f32[48]{0:T(128)}, f32[48]{0:T(128)}, /*index=5*/f32[48]{0:T(128)}, f32[3072]{0:T(1024)}), (f32[1536]{0:T(1024)}, ...) | async-done | bytes 85584 | tf_op jit(solution)/shard_map/psum | solution.py:177
  881.7 1.4 copy.197
  (191 shorter events, 41.2 us)
Async XLA Ops:
  7.2 121.1 %all-gather.3.cloned.1.call-start = ((), (), s32[]{:S(2)}) async-start(), calls=%async_computation.3 | async-start | bytes 20367360 | tf_op jit(solution)/shard_map/all_gather | solution.py:145
  7.9 204.3 %all-gather.5.cloned.1.call-start = ((), (), s32[]{:S(2)}) async-start(), calls=%async_computation.4 | async-start | bytes 9584640 | tf_op jit(solution)/shard_map/all_gather | solution.py:156
  8.7 445.0 %reduce-scatter.5.cloned.1.call-start = ((), (), s32[]{:S(2)}) async-start(), calls=%async_computation.5 | async-start | bytes 19169280 | tf_op jit(solution)/shard_map/reduce_scatter | solution.py:174
  11.8 129.2 %copy-start.19 = (f32[3328]{0:T(1024)}, f32[3328]{0:T(1024)S(1)}, u32[]{:S(2)}) copy-start(f32[3328]{0:T(1024)S(1)} %get-tuple-element.134) | copy-start | bytes 39940
  11.8 129.2 %copy-start.21 = (f32[3328]{0:T(1024)}, f32[3328]{0:T(1024)S(1)}, u32[]{:S(2)}) copy-start(f32[3328]{0:T(1024)S(1)} %get-tuple-element.135) | copy-start | bytes 39940
  11.8 129.2 %copy-start.23 = (f32[3328]{0:T(1024)}, f32[3328]{0:T(1024)S(1)}, u32[]{:S(2)}) copy-start(f32[3328]{0:T(1024)S(1)} %get-tuple-element.136) | copy-start | bytes 39940
  11.8 129.2 %copy-start.25 = (f32[3328]{0:T(1024)}, f32[3328]{0:T(1024)S(1)}, u32[]{:S(2)}) copy-start(f32[3328]{0:T(1024)S(1)} %get-tuple-element.137) | copy-start | bytes 39940
  13.2 115.0 %copy-start.50 = (f32[256]{0:T(256)}, f32[256]{0:T(256)S(1)}, u32[]{:S(2)}) copy-start(f32[256]{0:T(256)S(1)} %fusion.54) | copy-start | bytes 3076
  13.2 125.0 %copy-start.37 = (f32[256]{0:T(256)}, f32[256]{0:T(256)S(1)}, u32[]{:S(2)}) copy-start(f32[256]{0:T(256)S(1)} %fusion.86) | copy-start | bytes 3076
  14.6 126.4 %copy-start.40 = (f32[256]{0:T(256)}, f32[256]{0:T(256)S(1)}, u32[]{:S(2)}) copy-start(f32[256]{0:T(256)S(1)} %get-tuple-element.174) | copy-start | bytes 3076
  14.6 126.4 %copy-start.42 = (f32[256]{0:T(256)}, f32[256]{0:T(256)S(1)}, u32[]{:S(2)}) copy-start(f32[256]{0:T(256)S(1)} %get-tuple-element.175) | copy-start | bytes 3076
  14.6 126.4 %copy-start.44 = (f32[256]{0:T(256)}, f32[256]{0:T(256)S(1)}, u32[]{:S(2)}) copy-start(f32[256]{0:T(256)S(1)} %get-tuple-element.176) | copy-start | bytes 3076
  141.0 4.1 copy-start
  158.8 5.0 copy-start.8
  158.8 5.0 copy-start.16
  158.8 5.0 copy-start.31
  158.8 5.0 copy-start.35
  183.4 5.8 copy-start.12
  183.5 5.8 copy-start.27
  188.2 33.1 %copy-start.48 = (f32[256]{0:T(256)}, f32[256]{0:T(256)S(1)}, u32[]{:S(2)}) copy-start(f32[256]{0:T(256)S(1)} %fusion.87) | copy-start | bytes 3076
  197.5 535.0 %reduce-scatter.7.cloned.1.call-start = ((), (), s32[]{:S(2)}) async-start(), calls=%async_computation.6 | async-start | bytes 40734720
  212.2 9.1 %copy-start.3 = (f32[256,3072]{1,0:T(8,128)S(1)}, f32[256,3072]{1,0:T(8,128)}, u32[]{:S(2)}) copy-start(f32[256,3072]{1,0:T(8,128)} %copy-done.2) | copy-start | bytes 9437188
  212.2 9.1 %copy-start.7 = (f32[256,3072]{1,0:T(8,128)S(1)}, f32[256,3072]{1,0:T(8,128)}, u32[]{:S(2)}) copy-start(f32[256,3072]{1,0:T(8,128)} %copy.158) | copy-start | bytes 9437188
  212.2 9.1 %copy-start.28 = (f32[3072]{0:T(1024)S(1)}, f32[3072]{0:T(1024)}, u32[]{:S(2)}) copy-start(f32[3072]{0:T(1024)} %param.21) | copy-start | bytes 36868
  227.6 6.5 copy-start.36
  232.0 26.6 %copy-start.33 = (f32[256,48]{0,1:T(8,128)}, f32[256,48]{0,1:T(8,128)S(1)}, u32[]{:S(2)}) copy-start(f32[256,48]{0,1:T(8,128)S(1)} %copy.167) | copy-start | bytes 147460
  234.1 24.5 %copy-start.34 = (f32[256,48]{0,1:T(8,128)}, f32[256,48]{0,1:T(8,128)S(1)}, u32[]{:S(2)}) copy-start(f32[256,48]{0,1:T(8,128)S(1)} %copy.163) | copy-start | bytes 147460
  234.8 23.8 %copy-start.30 = (pred[256,256]{1,0:T(8,128)(4,1)}, pred[256,256]{1,0:T(8,128)(4,1)S(1)}, u32[]{:S(2)}) copy-start(pred[256,256]{1,0:T(8,128)(4,1)S(1)} %get-tuple-element.171) | copy-start | bytes 196612
  236.2 22.4 %copy-start.17 = (f32[256,256]{1,0:T(8,128)}, f32[256,256]{1,0:T(8,128)S(1)}, u32[]{:S(2)}) copy-start(f32[256,256]{1,0:T(8,128)S(1)} %fusion.104) | copy-start | bytes 786436
  236.2 22.8 %copy-start.14 = (f32[256,128]{1,0:T(8,128)S(1)}, f32[256,128]{1,0:T(8,128)}, u32[]{:S(2)}) copy-start(f32[256,128]{1,0:T(8,128)} %get-tuple-element.100) | copy-start | bytes 393220
  258.9 5.2 copy-start.13
  285.5 6.9 copy-start.32
  292.5 7.8 copy-start.6
  299.7 6.1 copy-start.47
  299.7 6.1 copy-start.54
  299.7 6.1 copy-start.55
  300.3 7.7 copy-start.5
  300.3 7.7 copy-start.11
  311.1 6.3 copy-start.20
  311.2 6.3 copy-start.22
  311.2 6.3 copy-start.24
  311.2 6.3 copy-start.26
  338.4 8.1 copy-start.56
  338.4 542.0 %all-reduce.22.cloned.1.call-start = ((), (), s32[]{:S(2)}) async-start(), calls=%async_computation.7 | async-start | bytes 183296 | tf_op jit(solution)/shard_map/psum | solution.py:177
  347.7 12.4 %copy-start.51 = (f32[256]{0:T(256)S(1)}, f32[256]{0:T(256)}, u32[]{:S(2)}) copy-start(f32[256]{0:T(256)} %copy-done.50) | copy-start | bytes 3076
  360.1 6.0 copy-start.4
  360.1 6.0 copy-start.29
  360.1 6.0 copy-start.49
  (14 other events, 29.6 us)
Sparse Core Ops, SparseCore 0:
  10.9 117.2 all-gather.2
  131.0 81.1 all-gather.4
  217.0 236.6 reduce-scatter.4
  459.4 273.1 reduce-scatter.6
  740.6 139.7 all-reduce.21
where the time goes:
time: 906 us; the launch traced here: 896 us
  waiting for transfers between devices  610 us (67%)
  matrix products  145 us (16%)
  other arithmetic  59.1 us (7%)
  local copies, waits for them, and re-layouts  58.8 us (6%)
  between operations  15.7 us (2%)
    unnamed x6, waiting for transfers between devices  279 us
    psum x1, waiting for transfers between devices, on_device(): lax.psum((grad_gain, grad_taps, grad_shift, grad_dt, grad_decay, grad_ski...  124 us
    all_gather x1, waiting for transfers between devices, on_device(): lax.all_gather(in_weight, 'shard', axis=0, tiled=True)  112 us
    reduce_scatter x1, waiting for transfers between devices, on_device(): lax.psum_scatter(local_out_grad, 'shard', scatter_dimension=0, tiled=True)  80 us
    dot_general x3, matrix products, block_step(): inside = jnp.einsum('tsh,shp->thp', weights, x_block, precision=highest)  52.2 us
    dot_general x2, matrix products, times_rows(): lax.dot_general(left, piece, (((1,), (1,)), ((), ())), preferred_element_...  20.8 us
    dot_general x1, matrix products, on_device(): lax.dot_general(normed_low, grad_proj_low, (((0,), (0,)), ((), ())), pref...  18.6 us
  transfers between devices with their start and end apart: 5, of which 5 were waited for; matrix products, arithmetic and copies ran while one was open for 28% of the time, Pallas kernels for 0%

commit v1 on v0

v1 whole, which is shorter than its diff:
```python
import functools

import jax
import jax.numpy as jnp
import numpy as np
from jax import lax
from jax.experimental import pallas as pl
from jax.experimental.pallas import tpu as pltpu
from jax.sharding import Mesh
from jax.sharding import PartitionSpec as P

LEN = 256
HALF = 128
HEAD = 64
GROUP = 8
WIDE = GROUP * HEAD
STATE = 128
TAPS = 4
NORM_EPS = 1e-05
LOG2E = 1.4426950408889634
FAR = -1e30
bf16 = jnp.bfloat16
f32 = jnp.float32
highest = lax.Precision.HIGHEST


def sigmoid(v):
    return 0.5 + 0.5 * jnp.tanh(0.5 * v)


def convolve(values, taps, bias, near):
    total = bias + taps[TAPS - 1 : TAPS] * values
    for back in range(1, TAPS):
        tap = taps[TAPS - 1 - back : TAPS - back]
        total = total + tap * (near[:, back : back + 1] * pltpu.roll(values, back, 0))
    return total


def convolve_back(grad, values, taps, near):
    total = taps[TAPS - 1 : TAPS] * grad
    rows = [jnp.sum(grad * values, axis=0, keepdims=True)]
    for back in range(1, TAPS):
        tap = taps[TAPS - 1 - back : TAPS - back]
        seen = near[:, back : back + 1] * grad
        total = total + tap * pltpu.roll(seen, LEN - back, 0)
        rows.append(jnp.sum(seen * pltpu.roll(values, back, 0), axis=0, keepdims=True))
    return total, rows[::-1] + [jnp.sum(grad, axis=0, keepdims=True)]


def silu_slope(v, s):
    return s * (1.0 + v * (1.0 - s))


def positions():
    return (
        lax.broadcasted_iota(jnp.int32, (LEN, LEN), 0),
        lax.broadcasted_iota(jnp.int32, (LEN, LEN), 1),
    )


def softplus(v):
    small = jnp.exp(-jnp.abs(v))
    return jnp.maximum(v, 0.0) + jnp.log1p(small)


def steps_of(dt_part, head_rows):
    raw = dt_part + head_rows[0:1]
    step = softplus(raw)
    rate = -step * head_rows[1:2]
    row, col = positions()
    lower = (row >= col).astype(f32)
    total = jnp.dot(lower, rate, precision=highest, preferred_element_type=f32) * LOG2E
    return raw, step, rate, total


def split_dot(values, ones):
    high = values.astype(bf16)
    low = (values - high.astype(f32)).astype(bf16)
    return jnp.dot(high, ones, preferred_element_type=f32) + jnp.dot(
        low, ones, preferred_element_type=f32
    )


def pair_columns(table, pair):
    lane = lax.broadcasted_iota(jnp.int32, (LEN, 2 * HEAD), 1)
    return jnp.where(lane < HEAD, table[:, 2 * pair : 2 * pair + 1], table[:, 2 * pair + 1 : 2 * pair + 2])


def halves(values):
    lane = lax.broadcasted_iota(jnp.int32, values.shape, 1)
    zero = jnp.zeros_like(values)
    return jnp.where(lane < HEAD, values, zero), jnp.where(lane >= HEAD, values, zero)


def mix_forward_kernel(
    proj_ref, shared_ref, near_ref, seg_col_ref, seg_row_ref, taps_ref, taps_shared_ref, head_ref,
    ssd_ref, scores, apart, totals, totals_row, steps,
):
    group = pl.program_id(1)
    near = near_ref[...]

    @pl.when(group == 0)
    def _():
        shared = shared_ref[...]
        mixed = convolve(shared[:, : 2 * STATE], taps_shared_ref[0:4], taps_shared_ref[4:5], near)
        mixed = mixed * sigmoid(mixed)
        b_low = mixed[:, :STATE].astype(bf16)
        c_low = mixed[:, STATE:].astype(bf16)
        scores[...] = lax.dot_general(
            c_low, b_low, (((1,), (1,)), ((), ())), preferred_element_type=f32
        )
        row, col = positions()
        seen = (row >= col) & (seg_col_ref[...] == seg_row_ref[0])
        apart[...] = jnp.where(seen, 0.0, FAR)
        raw, step, rate, total = steps_of(shared[:, 2 * STATE :], head_ref[...])
        for g in range(totals.shape[0]):
            turn = (STATE - GROUP * g) % STATE
            totals[g] = pltpu.roll(total, turn, 1) if turn else total
            steps[g] = pltpu.roll(step, turn, 1) if turn else step
        totals_row[...] = total.T

    values = proj_ref[...]
    mixed = convolve(values, taps_ref[0:4], taps_ref[4:5], near)
    x = mixed * sigmoid(mixed)
    total = totals[group]
    step = steps[group]
    total_row = totals_row[pl.ds(pl.multiple_of(group * GROUP, GROUP), GROUP), :]
    skip = taps_ref[5:6]
    for pair in range(GROUP // 2):
        lanes = slice(2 * HEAD * pair, 2 * HEAD * (pair + 1))
        x_pair = x[:, lanes]
        sides = halves((pair_columns(step, pair) * x_pair).astype(bf16))
        upper = lower = 0.0
        for side in range(2):
            head = 2 * pair + side
            col = total[:, head : head + 1]
            row = total_row[head : head + 1, :]
            decay = jnp.exp2(col[:HALF] - row[:, :HALF] + apart[:HALF, :HALF])
            weight = (scores[:HALF, :HALF] * decay).astype(bf16)
            upper = upper + jnp.dot(weight, sides[side][:HALF], preferred_element_type=f32)
            decay = jnp.exp2(col[HALF:] - row + apart[HALF:, :])
            weight = (scores[HALF:, :] * decay).astype(bf16)
            lower = lower + jnp.dot(weight, sides[side], preferred_element_type=f32)
        skipped = skip[:, lanes] * x_pair
        ssd_ref[:HALF, lanes] = upper + skipped[:HALF]
        ssd_ref[HALF:, lanes] = lower + skipped[HALF:]


def mix_backward_kernel(
    proj_ref, shared_ref, near_ref, seg_col_ref, seg_row_ref, taps_ref, taps_shared_ref, head_ref,
    ssd_ref, dssd_ref,
    dproj_ref, drows_ref, drows_shared_ref, dheads_ref,
    scores, apart, totals, totals_row, steps, b_keep, c_keep, dscores, dtotal, dstep,
):
    group = pl.program_id(1)
    last = pl.num_programs(1) - 1
    near = near_ref[...]

    @pl.when(group == 0)
    def _():
        shared = shared_ref[...]
        mixed = convolve(shared[:, : 2 * STATE], taps_shared_ref[0:4], taps_shared_ref[4:5], near)
        mixed = mixed * sigmoid(mixed)
        b_low = mixed[:, :STATE].astype(bf16)
        c_low = mixed[:, STATE:].astype(bf16)
        b_keep[...] = b_low
        c_keep[...] = c_low
        scores[...] = lax.dot_general(
            b_low, c_low, (((1,), (1,)), ((), ())), preferred_element_type=f32
        )
        row, col = positions()
        seen = (row <= col) & (seg_col_ref[...] == seg_row_ref[0])
        apart[...] = jnp.where(seen, 0.0, FAR)
        raw, step, rate, total = steps_of(shared[:, 2 * STATE :], head_ref[...])
        for g in range(totals.shape[0]):
            turn = (STATE - GROUP * g) % STATE
            totals[g] = pltpu.roll(total, turn, 1) if turn else total
            steps[g] = pltpu.roll(step, turn, 1) if turn else step
        totals_row[...] = total.T
        dscores[...] = jnp.zeros_like(dscores)
        dtotal[...] = jnp.zeros_like(dtotal)
        dstep[...] = jnp.zeros_like(dstep)

    values = proj_ref[...]
    mixed = convolve(values, taps_ref[0:4], taps_ref[4:5], near)
    gate = sigmoid(mixed)
    x = mixed * gate
    total = totals[group]
    step = steps[group]
    total_row = totals_row[pl.ds(pl.multiple_of(group * GROUP, GROUP), GROUP), :]
    skip = taps_ref[5:6]
    dx_parts, total_parts, step_parts, skip_parts = [], [], [], []
    for pair in range(GROUP // 2):
        lanes = slice(2 * HEAD * pair, 2 * HEAD * (pair + 1))
        x_pair = x[:, lanes]
        dt_pair = pair_columns(step, pair)
        low_x = (dt_pair * x_pair).astype(bf16)
        low_dy = dssd_ref[:, lanes]
        dy = low_dy.astype(f32)
        x_sides = halves(low_x)
        dy_sides = halves(low_dy)
        upper = lower = 0.0
        for side in range(2):
            head = 2 * pair + side
            col = total[:, head : head + 1]
            row = total_row[head : head + 1, :]
            decay = jnp.exp2(row - col[:HALF] + apart[:HALF, :])
            weight = (scores[:HALF, :] * decay).astype(bf16)
            upper = upper + jnp.dot(weight, dy_sides[side], preferred_element_type=f32)
            grad = lax.dot_general(
                x_sides[side][:HALF], low_dy, (((1,), (1,)), ((), ())), preferred_element_type=f32
            )
            dscores[:HALF, :] += grad * decay
            decay = jnp.exp2(row[:, HALF:] - col[HALF:] + apart[HALF:, HALF:])
            weight = (scores[HALF:, HALF:] * decay).astype(bf16)
            lower = lower + jnp.dot(weight, dy_sides[side][HALF:], preferred_element_type=f32)
            grad = lax.dot_general(
                x_sides[side][HALF:], low_dy[HALF:], (((1,), (1,)), ((), ())),
                preferred_element_type=f32,
            )
            dscores[HALF:, HALF:] += grad * decay
        back = jnp.concatenate([upper, lower], axis=0)
        skip_pair = skip[:, lanes]
        inside = ssd_ref[:, lanes] - skip_pair * x_pair
        total_parts.append(dy * inside - low_x.astype(f32) * back)
        step_parts.append(x_pair * back)
        skip_parts.append(jnp.sum(dy * x_pair, axis=0, keepdims=True))
        dx_parts.append(dt_pair * back + skip_pair * dy)
    wide = lambda parts: jnp.concatenate(parts, axis=1)
    place = lax.broadcasted_iota(jnp.int32, (WIDE, STATE), 0) // HEAD + group * GROUP
    ones = (place == lax.broadcasted_iota(jnp.int32, (WIDE, STATE), 1)).astype(bf16)
    dtotal[...] += split_dot(wide(total_parts), ones)
    dstep[...] += split_dot(wide(step_parts), ones)
    dmixed = wide(dx_parts) * silu_slope(mixed, gate)
    dvalues, rows = convolve_back(dmixed, values, taps_ref[0:4], near)
    dproj_ref[:, pl.ds(pl.multiple_of(group * WIDE, WIDE), WIDE)] = dvalues.astype(bf16)
    drows_ref[0] = jnp.concatenate(
        rows + [wide(skip_parts), jnp.zeros((2, WIDE), f32)], axis=0
    )

    @pl.when(group == last)
    def _():
        shared = shared_ref[...]
        values = shared[:, : 2 * STATE]
        mixed = convolve(values, taps_shared_ref[0:4], taps_shared_ref[4:5], near)
        gate = sigmoid(mixed)
        low = dscores[...].astype(bf16)
        db = jnp.dot(low, c_keep[...], preferred_element_type=f32)
        dc = lax.dot_general(
            low, b_keep[...], (((0,), (0,)), ((), ())), preferred_element_type=f32
        )
        dmixed = jnp.concatenate([db, dc], axis=1) * silu_slope(mixed, gate)
        dvalues, rows = convolve_back(dmixed, values, taps_shared_ref[0:4], near)
        drows_shared_ref[0] = jnp.concatenate(rows + [jnp.zeros((3, 2 * STATE), f32)], axis=0)
        raw, step, rate, total = steps_of(shared[:, 2 * STATE :], head_ref[...])
        row, col = positions()
        upper = (row <= col).astype(f32)
        drate = jnp.dot(upper, dtotal[...], precision=highest, preferred_element_type=f32)
        draw = (dstep[...] - drate * head_ref[1:2]) * sigmoid(raw)
        at = dproj_ref.shape[1] - 3 * STATE
        dproj_ref[:, at : at + 2 * STATE] = dvalues.astype(bf16)
        dproj_ref[:, at + 2 * STATE :] = draw.astype(bf16)
        dheads_ref[0] = jnp.concatenate(
            [
                jnp.sum(draw, axis=0, keepdims=True),
                jnp.sum(drate * rate, axis=0, keepdims=True),
                jnp.zeros((6, STATE), f32),
            ],
            axis=0,
        )


def mixer_specs(columns):
    return [
        pl.BlockSpec((LEN, WIDE), lambda s, g: (s, g)),
        pl.BlockSpec((LEN, 3 * STATE), lambda s, g: (s, columns // (3 * STATE))),
        pl.BlockSpec((LEN, 8), lambda s, g: (s, 0)),
        pl.BlockSpec((LEN, 1), lambda s, g: (s, 0)),
        pl.BlockSpec((1, 1, LEN), lambda s, g: (s, 0, 0)),
        pl.BlockSpec((8, WIDE), lambda s, g: (0, g)),
        pl.BlockSpec((8, 2 * STATE), lambda s, g: (0, 0)),
        pl.BlockSpec((8, STATE), lambda s, g: (0, 0)),
    ]


def mixer_scratch(groups):
    return [
        pltpu.VMEM((LEN, LEN), f32),
        pltpu.VMEM((LEN, LEN), f32),
        pltpu.VMEM((groups, LEN, STATE), f32),
        pltpu.VMEM((STATE, LEN), f32),
        pltpu.VMEM((groups, LEN, STATE), f32),
    ]


def mix_forward(proj, near, seg_col, seg_row, taps, taps_shared, heads):
    rows, columns = proj.shape[0], proj.shape[1] - 3 * STATE
    groups = columns // WIDE
    return pl.pallas_call(
        mix_forward_kernel,
        grid=(rows // LEN, groups),
        in_specs=mixer_specs(columns),
        out_specs=pl.BlockSpec((LEN, WIDE), lambda s, g: (s, g)),
        out_shape=jax.ShapeDtypeStruct((rows, columns), f32),
        scratch_shapes=mixer_scratch(groups),
        compiler_params=pltpu.CompilerParams(vmem_limit_bytes=32 * 2**20),
        cost_estimate=pl.CostEstimate(flops=10**9, bytes_accessed=8 * 2**20, transcendentals=10**7),
        name="mix_forward",
    )(proj, proj, near, seg_col, seg_row, taps, taps_shared, heads)


def mix_backward(proj, near, seg_col, seg_row, taps, taps_shared, heads, ssd, dssd):
    rows, columns = proj.shape[0], proj.shape[1] - 3 * STATE
    groups, seqs = columns // WIDE, rows // LEN
    wide = pl.BlockSpec((LEN, WIDE), lambda s, g: (s, g))
    return pl.pallas_call(
        mix_backward_kernel,
        grid=(seqs, groups),
        in_specs=mixer_specs(columns) + [wide, wide],
        out_specs=[
            pl.BlockSpec((LEN, columns + 3 * STATE), lambda s, g: (s, 0)),
            pl.BlockSpec((1, 8, WIDE), lambda s, g: (s, 0, g)),
            pl.BlockSpec((1, 8, 2 * STATE), lambda s, g: (s, 0, 0)),
            pl.BlockSpec((1, 8, STATE), lambda s, g: (s, 0, 0)),
        ],
        out_shape=[
            jax.ShapeDtypeStruct(proj.shape, bf16),
            jax.ShapeDtypeStruct((seqs, 8, columns), f32),
            jax.ShapeDtypeStruct((seqs, 8, 2 * STATE), f32),
            jax.ShapeDtypeStruct((seqs, 8, STATE), f32),
        ],
        scratch_shapes=mixer_scratch(groups)
        + [
            pltpu.VMEM((LEN, STATE), bf16),
            pltpu.VMEM((LEN, STATE), bf16),
            pltpu.VMEM((LEN, LEN), f32),
            pltpu.VMEM((LEN, STATE), f32),
            pltpu.VMEM((LEN, STATE), f32),
        ],
        compiler_params=pltpu.CompilerParams(vmem_limit_bytes=40 * 2**20),
        cost_estimate=pl.CostEstimate(flops=3 * 10**9, bytes_accessed=12 * 2**20, transcendentals=10**7),
        name="mix_backward",
    )(proj, proj, near, seg_col, seg_row, taps, taps_shared, heads, ssd, dssd)


def shifted(value, axis, by):
    size = lax.axis_size(axis)
    return lax.ppermute(value, axis, [(i, (i + by) % size) for i in range(size)])


def swapped(value):
    return lax.ppermute(value, "grp", [(0, 1), (1, 0)])


def in_order(own, other, axis=0):
    first = lax.axis_index("grp") == 0
    return jnp.concatenate([jnp.where(first, own, other), jnp.where(first, other, own)], axis=axis)


def turned(value, dim, by):
    twice = jnp.concatenate([value, value], axis=dim)
    return lax.dynamic_slice_in_dim(twice, by, value.shape[dim], dim)


def summed_over(value, axis):
    total = value
    for by in range(1, lax.axis_size(axis)):
        total = total + shifted(value, axis, by)
    return total


def scattered(pieces, axis):
    total = pieces[0]
    for by in range(1, len(pieces)):
        total = total + shifted(pieces[by].astype(bf16), axis, by).astype(f32)
    return total


def halved(array, size, dim):
    return lax.dynamic_slice_in_dim(array, lax.axis_index("grp") * size, size, dim)


def times(left, right):
    return jnp.dot(left, right, preferred_element_type=f32)


def times_turned(left, right):
    return lax.dot_general(left, right, (((1,), (1,)), ((), ())), preferred_element_type=f32)


CHIPS = ("z", "y", "x")
ORDERS = (("z", "y", "x"), ("y", "x", "z"), ("x", "z", "y"))


def on_device(
    tokens,
    segment_ids,
    norm_gain,
    in_weight,
    conv_weight,
    conv_bias,
    dt_bias,
    a_log,
    skip_d,
    gnorm_gain,
    out_weight,
    cotangent,
):
    width = tokens.shape[1]
    inner = gnorm_gain.shape[0]
    half = inner // 2
    heads = dt_bias.shape[0] // 2
    bc = conv_bias.shape[0] - inner
    rows_in, rows_out = in_weight.shape[0], out_weight.shape[0]

    w_dt = halved(in_weight[:, inner + inner + bc :], heads, 1)
    own_mix = jnp.concatenate(
        [
            halved(in_weight[:, inner : 2 * inner], half, 1),
            in_weight[:, 2 * inner : 2 * inner + bc],
            w_dt,
            jnp.zeros((rows_in, STATE - heads), bf16),
        ],
        axis=1,
    )
    own_gate = halved(in_weight[:, :inner], half, 1)
    own_out = halved(out_weight, width // 2, 1)
    w_mix = lax.all_gather(own_mix, CHIPS, axis=0, tiled=True)
    w_gate = lax.all_gather(own_gate, CHIPS, axis=0, tiled=True)
    w_out = lax.all_gather(own_out, CHIPS, axis=0, tiled=True)

    residual = tokens.astype(f32)
    scale = lax.rsqrt(jnp.mean(residual * residual, axis=-1, keepdims=True) + NORM_EPS)
    unit = residual * scale
    own_low = (unit * norm_gain).astype(bf16)
    normed = in_order(own_low, swapped(own_low))
    cot = in_order(cotangent, swapped(cotangent))
    segments = in_order(segment_ids, swapped(segment_ids))
    near = [jnp.zeros(segments.shape, f32)]
    for back in range(1, TAPS):
        same = (segments[:, back:] == segments[:, :-back]).astype(f32)
        near.append(jnp.pad(same, ((0, 0), (back, 0))))
    near = jnp.stack(near + [near[0]] * 4, axis=-1).reshape(-1, 8)
    seg_col = segments.astype(f32).reshape(-1, 1)
    seg_row = segments.astype(f32)[:, None, :]

    taps = jnp.concatenate(
        [
            halved(conv_weight[:, :inner], half, 1),
            halved(conv_bias[None, :inner], half, 1),
            jnp.repeat(halved(skip_d, heads, 0), HEAD)[None],
            jnp.zeros((2, half), f32),
        ]
    )
    taps_shared = jnp.concatenate(
        [conv_weight[:, inner:], conv_bias[None, inner:], jnp.zeros((3, bc), f32)]
    )
    head_rows = jnp.stack([halved(dt_bias, heads, 0), jnp.exp(halved(a_log, heads, 0))])
    head_rows = jnp.pad(head_rows, ((0, 6), (0, STATE - heads)))
    gain = halved(gnorm_gain, half, 0)

    turned_low = normed.T.reshape(4, 4, 4, rows_in, -1)
    for dim, axis in enumerate(CHIPS):
        turned_low = turned(turned_low, dim, lax.axis_index(axis))
    leaving = []
    for order in ORDERS:
        dims = tuple(CHIPS.index(axis) for axis in order)
        leaving.append(turned_low.transpose(dims + (3, 4)).reshape(4, 16 * rows_in, -1))

    proj = times(normed, w_mix)
    sides = (near, seg_col, seg_row, taps, taps_shared, head_rows)
    ssd = mix_forward(proj, *sides)
    gate_part = times(normed, w_gate)
    cot_half = halved(cot, width // 2, 1)
    mixer_parts = times_turned(cot_half, w_out).astype(bf16)
    core = lax.axis_index("grp")
    grad_mixer = halved(mixer_parts, half, 1).astype(f32) + swapped(
        lax.dynamic_slice_in_dim(mixer_parts, (1 - core) * half, half, 1)
    ).astype(f32)
    opened = sigmoid(gate_part)
    gate = gate_part * opened
    gated = ssd * gate
    weighted = grad_mixer * gain
    sums = jnp.stack([jnp.sum(gated * gated, axis=-1), jnp.sum(gated * weighted, axis=-1)])
    sums = sums + swapped(sums)
    gscale = lax.rsqrt(sums[0] / inner + NORM_EPS)[:, None]
    pull = gscale * gscale * gscale * (sums[1] / inner)[:, None]
    mixer_low = (gated * gscale * gain).astype(bf16)
    dgated = gscale * weighted - gated * pull
    grad_gain = jnp.sum(grad_mixer * gated * gscale, axis=0)
    dgate_low = (dgated * ssd * silu_slope(gate_part, opened)).astype(bf16)
    dssd = (dgated * gate).astype(bf16)
    mixer_other = swapped(mixer_low)
    mixer_all = in_order(mixer_low, mixer_other, axis=1)

    out_grad = lax.dot_general(
        mixer_all, cot_half, (((0,), (0,)), ((), ())), preferred_element_type=f32
    ).astype(bf16)
    gate_grad = times(normed.T, dgate_low).astype(bf16)
    out_share = lax.psum_scatter(out_grad, ("z", "y"), scatter_dimension=0, tiled=True)
    gate_share = lax.psum_scatter(gate_grad, ("z", "y"), scatter_dimension=0, tiled=True)

    dproj, drows, drows_shared, dheads = mix_backward(proj, *sides, ssd, dssd)
    mix_shares = []
    wide = dproj.shape[1] // 3
    for stream, order in enumerate(ORDERS):
        columns = dproj[:, stream * wide : (stream + 1) * wide]
        pieces = [times(leaving[stream][k], columns) for k in range(4)]
        share = scattered(pieces, order[0])
        share = scattered(list(share.reshape(4, 4 * rows_in, wide)), order[1])
        share = scattered(list(share.reshape(4, rows_in, wide)), order[2])
        mix_shares.append(share)
    mix_share = jnp.concatenate(mix_shares, axis=1)

    out_turned = turned(out_share.reshape(4, rows_out, -1), 0, lax.axis_index("x"))
    out_total = scattered([out_turned[0].astype(f32)] + list(out_turned[1:]), "x")
    gate_turned = turned(gate_share.reshape(4, rows_in, -1), 0, lax.axis_index("x"))
    gate_total = scattered([gate_turned[0].astype(f32)] + list(gate_turned[1:]), "x")

    out_part = times(mixer_all, w_out)
    out_own = halved(out_part, LEN, 0).astype(bf16)
    out_other = swapped(lax.dynamic_slice_in_dim(out_part, (1 - core) * LEN, LEN, 0).astype(bf16))
    branch = in_order(out_own, out_other, axis=1)
    out_tokens = (residual + branch.astype(f32)).astype(bf16)

    normed_part = times_turned(dproj, w_mix) + times_turned(dgate_low, w_gate)
    grad_normed = halved(normed_part, LEN, 0) + swapped(
        lax.dynamic_slice_in_dim(normed_part, (1 - core) * LEN, LEN, 0).astype(bf16)
    ).astype(f32)
    q = grad_normed * norm_gain
    grad_tokens = cotangent.astype(f32) + scale * (
        q - unit * jnp.mean(q * unit, axis=-1, keepdims=True)
    )
    grad_norm_gain = jnp.sum(grad_normed * unit, axis=0)

    drows, drows_shared, dheads = drows.sum(0), drows_shared.sum(0), dheads.sum(0)
    small = jnp.concatenate(
        [
            drows[:6],
            grad_gain[None],
            grad_norm_gain[None],
            jnp.concatenate([drows_shared[:5].reshape(1, -1), dheads[:2].reshape(1, -1)], axis=1),
        ]
    )
    for axis in CHIPS:
        small = summed_over(small, axis)

    small_other = swapped(small)
    mix_other, gate_other, out_other = swapped(mix_share), swapped(gate_total), swapped(out_total)
    bc_sum = (mix_share + mix_other)[:, half : half + bc]
    dt_at = slice(half + bc, half + bc + heads)
    grad_in_weight = jnp.concatenate(
        [
            in_order(gate_total, gate_other, axis=1),
            in_order(mix_share[:, :half], mix_other[:, :half], axis=1),
            bc_sum,
            in_order(mix_share[:, dt_at], mix_other[:, dt_at], axis=1),
        ],
        axis=1,
    )
    grad_out_weight = in_order(out_total, out_other, axis=1)
    both = in_order(small[:7], small_other[:7], axis=1)
    shared_sum = (small + small_other)[7:]
    shared_rows = shared_sum[1, : 5 * bc].reshape(5, bc)
    head_sums = in_order(
        small[8, 5 * bc :].reshape(2, STATE)[:, :heads],
        small_other[8, 5 * bc :].reshape(2, STATE)[:, :heads],
        axis=1,
    )
    return (
        out_tokens,
        grad_tokens,
        shared_sum[0],
        grad_in_weight,
        jnp.concatenate([both[:4], shared_rows[:4]], axis=1),
        jnp.concatenate([both[4], shared_rows[4]]),
        head_sums[0],
        head_sums[1],
        both[5].reshape(-1, HEAD).sum(axis=-1),
        both[6],
        grad_out_weight,
    )


def solution(mesh):
    chips = Mesh(mesh.devices.reshape(2, 4, 4, 4), ("grp",) + CHIPS)
    rows = P(("grp",) + CHIPS, None)
    owned = P(CHIPS, None)
    return jax.shard_map(
        on_device,
        mesh=chips,
        in_specs=(rows, rows, P(), owned, P(), P(), P(), P(), P(), P(), owned, rows),
        out_specs=(rows, rows, P(), owned, P(), P(), P(), P(), P(), P(), owned),
        check_vma=False,
    )
```

time: 906 us -> 476 us (0.53)
  waiting for transfers between devices: 610 us -> 229 us
  matrix products: 145 us -> 52.6 us
  starting transfers between devices: 0.2 us -> 77.6 us
  Pallas kernels: 0 us -> 27.9 us
  other arithmetic: 59.1 us -> 32.2 us
  local copies, waits for them, and re-layouts: 58.8 us -> 32.8 us
    unnamed x6 -> x5, waiting for transfers between devices: 279 us -> 0.11 us
    psum x1 -> x0, waiting for transfers between devices: 124 us -> none  [on_device(): lax.psum((grad_gain, grad_taps, grad_shift, grad_dt, grad_decay, grad_ski...]
    dot_general x18 -> x20, matrix products: 145 us -> 52.6 us  [the longest x16 34.7 us: times(): return jnp.dot(left, right, preferred_element_type=f32)]
    ppermute x0 -> x54, starting transfers between devices: none -> 77.4 us  [the longest x42 53.5 us: shifted(): lax.ppermute(value, axis, [(i, (i + by) % size) for i in range(size)])]
    reduce_scatter x1 -> x2, waiting for transfers between devices: 80 us -> 3.39 us  [the longest x1 3.39 us: on_device(): lax.psum_scatter(out_grad, ('z', 'y'), scatter_dimension=0, tiled=True)]
    ppermute x0 -> x54, waiting for transfers between devices: none -> 49.6 us  [the longest x42 46 us: shifted(): lax.ppermute(value, axis, [(i, (i + by) % size) for i in range(size)])]
    all_gather x2 -> x3, waiting for transfers between devices: 127 us -> 176 us  [the longest x1 62 us: on_device(): w_out = lax.all_gather(own_out, CHIPS, axis=0, tiled=True)]
    pallas_call x0 -> x2, Pallas kernels: none -> 27.9 us  [the longest x1 18.7 us: mix_backward(): pl.pallas_call(mix_backward_kernel, grid=(seqs, groups), in_specs=mixer_s...]
  transfers between devices with their start and end apart: 5 -> 59, of which waited for: 5 -> 23; matrix products, arithmetic and copies ran while one was open for 28% -> 18% of each run, Pallas kernels for 0% -> 6%
where the time goes in v1:
time: 476 us; the launch traced here: 467 us
  waiting for transfers between devices  229 us (48%)
  starting transfers between devices  77.6 us (16%)
  matrix products  52.6 us (11%)
  local copies, waits for them, and re-layouts  32.8 us (7%)
  other arithmetic  32.2 us (7%)
  Pallas kernels  27.9 us (6%)
  between operations  15.4 us (3%)
    all_gather x1, waiting for transfers between devices, on_device(): w_out = lax.all_gather(own_out, CHIPS, axis=0, tiled=True)  62 us
    all_gather x1, waiting for transfers between devices, on_device(): w_mix = lax.all_gather(own_mix, CHIPS, axis=0, tiled=True)  60 us
    all_gather x1, waiting for transfers between devices, on_device(): w_gate = lax.all_gather(own_gate, CHIPS, axis=0, tiled=True)  53.7 us
    ppermute x42, starting transfers between devices, shifted(): lax.ppermute(value, axis, [(i, (i + by) % size) for i in range(size)])  53.5 us
    ppermute x42, waiting for transfers between devices, shifted(): lax.ppermute(value, axis, [(i, (i + by) % size) for i in range(size)])  46 us
    dot_general x16, matrix products, times(): return jnp.dot(left, right, preferred_element_type=f32)  34.7 us
    ppermute x12, starting transfers between devices, swapped(): return lax.ppermute(value, 'grp', [(0, 1), (1, 0)])  23.9 us
    pallas_call x1, Pallas kernels, mix_backward(): pl.pallas_call(mix_backward_kernel, grid=(seqs, groups), in_specs=mixer_s...  18.7 us
  transfers between devices with their start and end apart: 59, of which 23 were waited for; matrix products, arithmetic and copies ran while one was open for 18% of the time, Pallas kernels for 6%

profile of v1, /device:TPU:1, one launch (start us, length us, event | category | flops | bytes accessed | tf_op | source)
XLA Modules:
  0.0 467.2 jit_solution(12085134127338907448)
XLA Ops:
  16.8 1.8 collective-permute-done.2
  18.6 2.1 broadcast_select_fusion.2
  20.7 62.0 %all-gather.8.cloned.1.call-done = bf16[3072,768]{1,0:T(8,128)(2,1)} async-done(((bf16[48,768]{1,0:T(8,128)(2,1)}), bf16[3072,768]{1,0:T(8,128)(2,1)}) %all-gather.8.cloned.1.call-update) | async-done | bytes 4718608 | tf_op jit(solution)/shard_map/all_gather | solution.py:430
  82.7 5.1 %convolution_convert_fusion.2 = bf16[512,3072]{1,0:T(8,128)(2,1)S(1)} fusion(bf16[3072,768]{1,0:T(8,128)(2,1)} %all-gather.8.cloned.1.call-done, s32[]{:T(128)S(6)} %select_n.176, bf16[256,1536]{1,0:T(8,128)(2,1)} %get-tuple-element.54, bf16[256,1536]{1,0:T(8,128)(2,1)S(1)} %get-tuple-element.53), kind=kOutput, calls=%fused_computation.2 | convolution fusion | flops 2419064832 | bytes 9437188 | tf_op jit(solution)/shard_map/dot_general | solution.py:388
  90.7 2.3 collective-permute-start.3
  95.8 60.0 %all-gather.4.cloned.1.call-done = bf16[1536,1920]{1,0:T(8,128)(2,1)} async-done(((bf16[24,1920]{1,0:T(8,128)(2,1)}), bf16[1536,1920]{1,0:T(8,128)(2,1)}) %all-gather.4.cloned.1.call-update) | async-done | bytes 5898256 | tf_op jit(solution)/shard_map/all_gather | solution.py:428
  155.8 5.6 %fusion.79.proj_ref.shared_ref = f32[512,1920]{1,0:T(8,128)S(1)} fusion(bf16[1536,1920]{1,0:T(8,128)(2,1)} %all-gather.4.cloned.1.call-done, bf16[256,1536]{1,0:T(8,128)(2,1)S(1)} %get-tuple-element.56, bf16[256,1536]{1,0:T(8,128)(2,1)S(1)} %get-tuple-element.55), kind=kOutput, calls=%fused_computation.221 | convolution fusion | flops 3023044608 | bytes 11403264 | tf_op jit(solution)/shard_map/dot_general | solution.py:384
  161.4 9.1 %mix_forward.1.ssd_ref = f32[512,1536]{1,0:T(8,128)S(1)} custom-call(f32[512,1920]{1,0:T(8,128)S(1)} %fusion.79.proj_ref.shared_ref, f32[512,1920]{1,0:T(8,128)S(1)} %fusion.79.proj_ref.shared_ref, f32[512,8]{1,0:T(8,128)S(1)} %copy.33.near_ref, f32[512,1]{1,0:T(8,128)S(1)} %bitcast.110, f32[2,1,256]{2,1,0:T(1,128)S(1)} %add_convert_fusion.seg_row_ref, ...), custom_call_target="tpu_custom_call" | custom-call | flops 1000000000 | bytes 8388608 | tf_op jit(solution)/shard_map/mix_forward/pallas_call | solution.py:299
  170.6 1.9 copy-done.15
  172.5 53.7 %all-gather.6.cloned.1.call-done = bf16[1536,1536]{1,0:T(8,128)(2,1)} async-done(((bf16[24,1536]{1,0:T(8,128)(2,1)}), bf16[1536,1536]{1,0:T(8,128)(2,1)}) %all-gather.6.cloned.1.call-update) | async-done | bytes 4718608 | tf_op jit(solution)/shard_map/all_gather | solution.py:429
  226.2 8.6 %multiply_reduce_fusion.2 = (f32[512]{0:T(512)S(1)}, f32[512]{0:T(512)S(1)}, f32[512,1536]{1,0:T(8,128)}) fusion(f32[512,1536]{1,0:T(8,128)S(1)} %mix_forward.1.ssd_ref, f32[1536]{0:T(1024)S(1)} %dynamic_slice.78, bf16[512,1536]{1,0:T(8,128)(2,1)} %collective-permute-done.3, bf16[512,3072]{1,0:T(8,128)(2,1)} %copy-done.30, s32[]{:T(128)S(6)} %select_n.169, ...), kind=kOutput, calls=%fused_computation.18 | convolution fusion | flops 2429287424 | bytes 15738884 | tf_op jit(solution)/shard_map/dot_general | solution.py:384
  234.8 2.9 collective-permute-start.4
  238.9 2.6 copy.37
  241.6 6.9 %multiply_convert_fusion = (bf16[512,1536]{1,0:T(8,128)(2,1)S(1)}, bf16[512,1536]{1,0:T(8,128)(2,1)}, f32[1536]{0:T(1024)}, bf16[512,1536]{1,0:T(8,128)(2,1)}) fusion(f32[512,1536]{1,0:T(8,128)} %get-tuple-element.108, f32[512,1536]{1,0:T(8,128)S(1)} %mix_forward.1.ssd_ref, f32[512]{0:T(512)S(1)} %fusion.68, bf16[512,1536]{1,0:T(8,128)(2,1)} %collective-permute-done.3, ...), kind=kLoop, calls=%fused_computation.12 | loop fusion | flops 21232128 | bytes 14172164 | tf_op jit(solution)/shard_map/convert_element_type | solution.py:491
  249.7 4.2 convolution_convert_fusion
  254.0 2.0 fusion.18
  265.5 18.7 %mix_backward.1 = (bf16[512,1920]{1,0:T(8,128)(2,1)S(1)}, f32[2,8,1536]{2,1,0:T(8,128)S(1)}, f32[2,8,256]{2,1,0:T(8,128)S(1)}, f32[2,8,128]{2,1,0:T(8,128)S(1)}) custom-call(f32[512,1920]{1,0:T(8,128)S(1)} %copy-done.16, f32[512,1920]{1,0:T(8,128)S(1)} %copy-done.16, f32[512,8]{1,0:T(8,128)S(1)} %copy.33.near_ref, f32[512,1]{1,0:T(8,128)S(1)} %bitcast.111, ...), custom_call_target="tpu_custom_call" | custom-call | flops 3000000000 | bytes 12582912 | tf_op jit(solution)/shard_map/mix_backward/pallas_call | solution.py:316
  290.8 1.7 convolution_convert_fusion.11
  292.7 1.7 convolution_convert_fusion.10
  294.4 2.3 collective-permute-start.23
  299.9 2.5 collective-permute-start.32
  303.4 5.8 %fusion.101 = f32[512,1536]{1,0:T(8,128)S(1)} fusion(bf16[512,1920]{1,0:T(8,128)(2,1)S(1)} %copy-done.3, bf16[1536,1920]{1,0:T(8,128)(2,1)} %all-gather.4.cloned.1.call-done), kind=kOutput, calls=%fused_computation.238 | convolution fusion | flops 3019898880 | bytes 11010048 | tf_op jit(solution)/shard_map/dot_general | solution.py:388
  309.2 2.6 convolution_add_fusion
  313.7 7.5 %collective-permute-done.23 = bf16[384,640]{1,0:T(8,128)(2,1)S(1)} collective-permute-done((bf16[384,640]{1,0:T(8,128)(2,1)S(1)}, bf16[384,640]{1,0:T(8,128)(2,1)S(1)}, u32[]{:S(2)}, u32[]{:S(2)}) %collective-permute-start.23) | collective-permute-done | bytes 491552 | tf_op jit(solution)/shard_map/ppermute | solution.py:348
  329.8 8.9 %collective-permute-done.40 = bf16[384,640]{1,0:T(8,128)(2,1)S(1)} collective-permute-done((bf16[384,640]{1,0:T(8,128)(2,1)S(1)}, bf16[384,640]{1,0:T(8,128)(2,1)S(1)}, u32[]{:S(2)}, u32[]{:S(2)}) %collective-permute-start.40) | collective-permute-done | bytes 491552 | tf_op jit(solution)/shard_map/ppermute | solution.py:348
  338.7 8.2 %collective-permute-done.41 = bf16[384,640]{1,0:T(8,128)(2,1)S(1)} collective-permute-done((bf16[384,640]{1,0:T(8,128)(2,1)S(1)}, bf16[384,640]{1,0:T(8,128)(2,1)S(1)}, u32[]{:S(2)}, u32[]{:S(2)}) %collective-permute-start.41) | collective-permute-done | bytes 491552 | tf_op jit(solution)/shard_map/ppermute | solution.py:348
  346.9 3.0 collective-permute-start.26
  353.3 1.7 collective-permute-start.35
  359.4 4.4 convolution_convert_fusion.1
  363.9 3.0 collective-permute-start.44
  375.1 2.3 collective-permute-start.39
  377.4 2.3 collective-permute-start.46
  382.6 2.0 collective-permute-done.47
  384.6 5.2 %collective-permute-start.49 = (f32[24,1920]{1,0:T(8,128)S(1)}, f32[24,1920]{1,0:T(8,128)S(1)}, u32[]{:S(2)}, u32[]{:S(2)}) collective-permute-start(f32[24,1920]{1,0:T(8,128)S(1)} %pad_maximum_fusion.5), channel_id=1, source_target_pairs={{0,64},{64,0},{1,65},{65,1},{2,66},{66,2},{3,67},{67,3},{4,68},{68... | collective-permute-start | bytes 552968 | tf_op jit(solution)/shard_map/ppermute | solution.py:352
  389.8 2.1 fusion.13
  394.7 2.5 collective-permute-done.10
  398.0 4.7 %collective-permute-done.9 = f32[9,1536]{1,0:T(8,128)S(1)} collective-permute-done((f32[9,1536]{1,0:T(8,128)S(1)}, f32[9,1536]{1,0:T(8,128)S(1)}, u32[]{:S(2)}, u32[]{:S(2)}) %collective-permute-start.9) | collective-permute-done | bytes 55328 | tf_op jit(solution)/shard_map/ppermute | solution.py:348
  402.8 3.7 collective-permute-start.12
  406.5 3.1 collective-permute-done.11
  409.6 3.5 collective-permute-done.12
  420.0 3.7 collective-permute-start.17
  427.9 6.0 %fusion.7 = bf16[512,768]{1,0:T(8,128)(2,1)S(1)} fusion(bf16[3072,768]{1,0:T(8,128)(2,1)} %all-gather.8.cloned.1.call-done, bf16[512,1536]{1,0:T(8,128)(2,1)} %copy-done.32, bf16[512,1536]{1,0:T(8,128)(2,1)} %copy-done.31), kind=kOutput, calls=%fused_computation.30 | convolution fusion | flops 2422210560 | bytes 8650752 | tf_op jit(solution)/shard_map/dot_general | solution.py:384
  436.1 2.1 fusion.12
  440.2 2.7 collective-permute-start.19
  443.0 3.4 reduce-scatter.5.cloned.1.call-done
  448.7 2.4 collective-permute-start.51
  452.4 3.2 collective-permute-start.21
  455.6 2.8 collective-permute-start.53
  (367 shorter events, 91.3 us)
Async XLA Ops:
  7.2 75.5 %all-gather.8.cloned.1.call-start = ((), (), s32[]{:S(2)}) async-start(), calls=%async_computation.4 | async-start | bytes 4792320 | tf_op jit(solution)/shard_map/all_gather | solution.py:430
  8.8 147.0 %all-gather.4.cloned.1.call-start = ((), (), s32[]{:S(2)}) async-start(), calls=%async_computation.2 | async-start | bytes 5990400 | tf_op jit(solution)/shard_map/all_gather | solution.py:428
  12.2 214.0 %all-gather.6.cloned.1.call-start = ((), (), s32[]{:S(2)}) async-start(), calls=%async_computation.3 | async-start | bytes 4792320 | tf_op jit(solution)/shard_map/all_gather | solution.py:429
  12.9 425.3 %reduce-scatter.3.cloned.1.call-start = ((), (), s32[]{:S(2)}) async-start(), calls=%async_computation.5 | async-start | bytes 5013504 | tf_op jit(solution)/shard_map/reduce_scatter | solution.py:501
  15.0 79.2 %collective-permute-start = (bf16[256,1536]{1,0:T(8,128)(2,1)S(1)}, bf16[256,1536]{1,0:T(8,128)(2,1)}, u32[]{:S(2)}, u32[]{:S(2)}) collective-permute-start(bf16[256,1536]{1,0:T(8,128)(2,1)S(1)} %fusion.8), channel_id=1, source_target_pairs={{0,64},{64,0},{1,65},{65,1},{2,66},{66,2},{3,67},{67,3},{4,68},{68... | collective-permute-start | bytes 2359304 | tf_op jit(solution)/shard_map/ppermute | solution.py:352
  90.7 135.5 %collective-permute-start.3 = (bf16[512,1536]{1,0:T(8,128)(2,1)}, bf16[512,1536]{1,0:T(8,128)(2,1)}, u32[]{:S(2)}, u32[]{:S(2)}) collective-permute-start(bf16[512,1536]{1,0:T(8,128)(2,1)} %constant_dynamic-slice_fusion), channel_id=1, source_target_pairs={{0,64},{64,0},{1,65},{65,1},{2,66},{66,2},{3,67},{67,3},{4,68},{68... | collective-permute-start | bytes 4718600 | tf_op jit(solution)/shard_map/ppermute | solution.py:352
  234.8 6.7 %collective-permute-start.4 = (f32[2,512]{1,0:T(2,128)S(1)}, f32[2,512]{1,0:T(2,128)S(1)}, u32[]{:S(2)}, u32[]{:S(2)}) collective-permute-start(f32[2,512]{1,0:T(2,128)S(1)} %pad_maximum_fusion.9), channel_id=1, source_target_pairs={{0,64},{64,0},{1,65},{65,1},{2,66},{66,2},{3,67},{67,3},{4,68},{68... | collective-permute-start | bytes 12296 | tf_op jit(solution)/shard_map/ppermute | solution.py:352
  253.9 192.4 %reduce-scatter.5.cloned.1.call-start = ((), (), s32[]{:S(2)}) async-start(), calls=%async_computation.6 | async-start | bytes 5013504 | tf_op jit(solution)/shard_map/reduce_scatter | solution.py:500
  292.5 20.4 %collective-permute-start.22 = (bf16[384,640]{1,0:T(8,128)(2,1)S(1)}, bf16[384,640]{1,0:T(8,128)(2,1)S(1)}, u32[]{:S(2)}, u32[]{:S(2)}) collective-permute-start(bf16[384,640]{1,0:T(8,128)(2,1)S(1)} %convolution_convert_fusion.11), channel_id=1, source_target_pairs={{0,16},{16,32},{32,48},{48,0},{1,17},{17,33},{33,49},{49,1},{2,18}... | collective-permute-start | bytes 1474568 | tf_op jit(solution)/shard_map/ppermute | solution.py:348
  294.4 26.8 %collective-permute-start.23 = (bf16[384,640]{1,0:T(8,128)(2,1)S(1)}, bf16[384,640]{1,0:T(8,128)(2,1)S(1)}, u32[]{:S(2)}, u32[]{:S(2)}) collective-permute-start(bf16[384,640]{1,0:T(8,128)(2,1)S(1)} %convolution_convert_fusion.10), channel_id=1, source_target_pairs={{0,32},{16,48},{32,0},{48,16},{1,33},{17,49},{33,1},{49,17},{2,34}... | collective-permute-start | bytes 1474568 | tf_op jit(solution)/shard_map/ppermute | solution.py:348
  297.2 24.9 %collective-permute-start.24 = (bf16[384,640]{1,0:T(8,128)(2,1)S(1)}, bf16[384,640]{1,0:T(8,128)(2,1)S(1)}, u32[]{:S(2)}, u32[]{:S(2)}) collective-permute-start(bf16[384,640]{1,0:T(8,128)(2,1)S(1)} %convolution_convert_fusion.9), channel_id=1, source_target_pairs={{0,48},{16,0},{32,16},{48,32},{1,49},{17,1},{33,17},{49,33},{2,50}... | collective-permute-start | bytes 1474568 | tf_op jit(solution)/shard_map/ppermute | solution.py:348
  298.8 24.6 %collective-permute-start.31 = (bf16[384,640]{1,0:T(8,128)(2,1)S(1)}, bf16[384,640]{1,0:T(8,128)(2,1)S(1)}, u32[]{:S(2)}, u32[]{:S(2)}) collective-permute-start(bf16[384,640]{1,0:T(8,128)(2,1)S(1)} %convolution_convert_fusion.8), channel_id=1, source_target_pairs={{0,4},{4,8},{8,12},{12,0},{1,5},{5,9},{9,13},{13,1},{2,6},{6,10},{... | collective-permute-start | bytes 1474568 | tf_op jit(solution)/shard_map/ppermute | solution.py:348
  299.9 25.0 %collective-permute-start.32 = (bf16[384,640]{1,0:T(8,128)(2,1)S(1)}, bf16[384,640]{1,0:T(8,128)(2,1)S(1)}, u32[]{:S(2)}, u32[]{:S(2)}) collective-permute-start(bf16[384,640]{1,0:T(8,128)(2,1)S(1)} %convolution_convert_fusion.7), channel_id=1, source_target_pairs={{0,8},{4,12},{8,0},{12,4},{1,9},{5,13},{9,1},{13,5},{2,10},{6,14},... | collective-permute-start | bytes 1474568 | tf_op jit(solution)/shard_map/ppermute | solution.py:348
  312.9 13.5 %collective-permute-start.33 = (bf16[384,640]{1,0:T(8,128)(2,1)S(1)}, bf16[384,640]{1,0:T(8,128)(2,1)S(1)}, u32[]{:S(2)}, u32[]{:S(2)}) collective-permute-start(bf16[384,640]{1,0:T(8,128)(2,1)S(1)} %convolution_convert_fusion.6), channel_id=1, source_target_pairs={{0,12},{4,0},{8,4},{12,8},{1,13},{5,1},{9,5},{13,9},{2,14},{6,2},{... | collective-permute-start | bytes 1474568 | tf_op jit(solution)/shard_map/ppermute | solution.py:348
  321.2 35.5 %collective-permute-start.5 = (bf16[512,1536]{1,0:T(8,128)(2,1)S(1)}, bf16[512,1536]{1,0:T(8,128)(2,1)S(1)}, u32[]{:S(2)}, u32[]{:S(2)}) collective-permute-start(bf16[512,1536]{1,0:T(8,128)(2,1)S(1)} %copy-done.19), channel_id=1, source_target_pairs={{0,64},{64,0},{1,65},{65,1},{2,66},{66,2},{3,67},{67,3},{4,68},{68... | collective-permute-start | bytes 4718600 | tf_op jit(solution)/shard_map/ppermute | solution.py:352
  322.2 67.6 %collective-permute-start.7 = (bf16[256,1536]{1,0:T(8,128)(2,1)S(1)}, bf16[256,1536]{1,0:T(8,128)(2,1)S(1)}, u32[]{:S(2)}, u32[]{:S(2)}) collective-permute-start(bf16[256,1536]{1,0:T(8,128)(2,1)S(1)} %dynamic-slice_convert_fusion), channel_id=1, source_target_pairs={{0,64},{64,0},{1,65},{65,1},{2,66},{66,2},{3,67},{67,3},{4,68},{68... | collective-permute-start | bytes 2359304 | tf_op jit(solution)/shard_map/ppermute | solution.py:352
  323.4 15.3 %collective-permute-start.40 = (bf16[384,640]{1,0:T(8,128)(2,1)S(1)}, bf16[384,640]{1,0:T(8,128)(2,1)S(1)}, u32[]{:S(2)}, u32[]{:S(2)}) collective-permute-start(bf16[384,640]{1,0:T(8,128)(2,1)S(1)} %convolution_convert_fusion.5), channel_id=1, source_target_pairs={{0,1},{1,2},{2,3},{3,0},{4,5},{5,6},{6,7},{7,4},{8,9},{9,10},{10,1... | collective-permute-start | bytes 1474568 | tf_op jit(solution)/shard_map/ppermute | solution.py:348
  324.9 22.0 %collective-permute-start.41 = (bf16[384,640]{1,0:T(8,128)(2,1)S(1)}, bf16[384,640]{1,0:T(8,128)(2,1)S(1)}, u32[]{:S(2)}, u32[]{:S(2)}) collective-permute-start(bf16[384,640]{1,0:T(8,128)(2,1)S(1)} %convolution_convert_fusion.4), channel_id=1, source_target_pairs={{0,2},{1,3},{2,0},{3,1},{4,6},{5,7},{6,4},{7,5},{8,10},{9,11},{10,... | collective-permute-start | bytes 1474568 | tf_op jit(solution)/shard_map/ppermute | solution.py:348
  326.3 23.6 %collective-permute-start.42 = (bf16[384,640]{1,0:T(8,128)(2,1)S(1)}, bf16[384,640]{1,0:T(8,128)(2,1)S(1)}, u32[]{:S(2)}, u32[]{:S(2)}) collective-permute-start(bf16[384,640]{1,0:T(8,128)(2,1)S(1)} %convolution_convert_fusion.3), channel_id=1, source_target_pairs={{0,3},{1,0},{2,1},{3,2},{4,7},{5,4},{6,5},{7,6},{8,11},{9,8},{10,9... | collective-permute-start | bytes 1474568 | tf_op jit(solution)/shard_map/ppermute | solution.py:348
  338.7 13.9 %collective-permute-start.25 = (bf16[96,640]{1,0:T(8,128)(2,1)S(1)}, bf16[96,640]{1,0:T(8,128)(2,1)S(1)}, u32[]{:S(2)}, u32[]{:S(2)}) collective-permute-start(bf16[96,640]{1,0:T(8,128)(2,1)S(1)} %get-tuple-element.61), channel_id=1, source_target_pairs={{0,4},{4,8},{8,12},{12,0},{1,5},{5,9},{9,13},{13,1},{2,6},{6,10},{... | collective-permute-start | bytes 368648 | tf_op jit(solution)/shard_map/ppermute | solution.py:348
  346.9 6.5 %collective-permute-start.26 = (bf16[96,640]{1,0:T(8,128)(2,1)S(1)}, bf16[96,640]{1,0:T(8,128)(2,1)S(1)}, u32[]{:S(2)}, u32[]{:S(2)}) collective-permute-start(bf16[96,640]{1,0:T(8,128)(2,1)S(1)} %get-tuple-element.63), channel_id=1, source_target_pairs={{0,8},{4,12},{8,0},{12,4},{1,9},{5,13},{9,1},{13,5},{2,10},{6,14},... | collective-permute-start | bytes 368648 | tf_op jit(solution)/shard_map/ppermute | solution.py:348
  349.9 5.5 %collective-permute-start.27 = (bf16[96,640]{1,0:T(8,128)(2,1)S(1)}, bf16[96,640]{1,0:T(8,128)(2,1)S(1)}, u32[]{:S(2)}, u32[]{:S(2)}) collective-permute-start(bf16[96,640]{1,0:T(8,128)(2,1)S(1)} %get-tuple-element.62), channel_id=1, source_target_pairs={{0,12},{4,0},{8,4},{12,8},{1,13},{5,1},{9,5},{13,9},{2,14},{6,2},{... | collective-permute-start | bytes 368648 | tf_op jit(solution)/shard_map/ppermute | solution.py:348
  352.6 11.3 %collective-permute-start.34 = (bf16[96,640]{1,0:T(8,128)(2,1)}, bf16[96,640]{1,0:T(8,128)(2,1)S(1)}, u32[]{:S(2)}, u32[]{:S(2)}) collective-permute-start(bf16[96,640]{1,0:T(8,128)(2,1)} %get-tuple-element.64), channel_id=1, source_target_pairs={{0,1},{1,2},{2,3},{3,0},{4,5},{5,6},{6,7},{7,4},{8,9},{9,10},{10,1... | collective-permute-start | bytes 368648 | tf_op jit(solution)/shard_map/ppermute | solution.py:348
  353.3 13.5 %collective-permute-start.35 = (bf16[96,640]{1,0:T(8,128)(2,1)}, bf16[96,640]{1,0:T(8,128)(2,1)S(1)}, u32[]{:S(2)}, u32[]{:S(2)}) collective-permute-start(bf16[96,640]{1,0:T(8,128)(2,1)} %get-tuple-element.66), channel_id=1, source_target_pairs={{0,2},{1,3},{2,0},{3,1},{4,6},{5,7},{6,4},{7,5},{8,10},{9,11},{10,... | collective-permute-start | bytes 368648 | tf_op jit(solution)/shard_map/ppermute | solution.py:348
  355.4 11.4 %collective-permute-start.36 = (bf16[96,640]{1,0:T(8,128)(2,1)}, bf16[96,640]{1,0:T(8,128)(2,1)S(1)}, u32[]{:S(2)}, u32[]{:S(2)}) collective-permute-start(bf16[96,640]{1,0:T(8,128)(2,1)} %get-tuple-element.65), channel_id=1, source_target_pairs={{0,3},{1,0},{2,1},{3,2},{4,7},{5,4},{6,5},{7,6},{8,11},{9,8},{10,9... | collective-permute-start | bytes 368648 | tf_op jit(solution)/shard_map/ppermute | solution.py:348
  356.7 12.6 %collective-permute-start.43 = (bf16[96,640]{1,0:T(8,128)(2,1)S(1)}, bf16[96,640]{1,0:T(8,128)(2,1)S(1)}, u32[]{:S(2)}, u32[]{:S(2)}) collective-permute-start(bf16[96,640]{1,0:T(8,128)(2,1)S(1)} %get-tuple-element.67), channel_id=1, source_target_pairs={{0,16},{16,32},{32,48},{48,0},{1,17},{17,33},{33,49},{49,1},{2,18}... | collective-permute-start | bytes 368648 | tf_op jit(solution)/shard_map/ppermute | solution.py:348
  363.9 7.0 %collective-permute-start.44 = (bf16[96,640]{1,0:T(8,128)(2,1)S(1)}, bf16[96,640]{1,0:T(8,128)(2,1)S(1)}, u32[]{:S(2)}, u32[]{:S(2)}) collective-permute-start(bf16[96,640]{1,0:T(8,128)(2,1)S(1)} %get-tuple-element.69), channel_id=1, source_target_pairs={{0,32},{16,48},{32,0},{48,16},{1,33},{17,49},{33,1},{49,17},{2,34}... | collective-permute-start | bytes 368648 | tf_op jit(solution)/shard_map/ppermute | solution.py:348
  366.9 5.6 %collective-permute-start.45 = (bf16[96,640]{1,0:T(8,128)(2,1)S(1)}, bf16[96,640]{1,0:T(8,128)(2,1)S(1)}, u32[]{:S(2)}, u32[]{:S(2)}) collective-permute-start(bf16[96,640]{1,0:T(8,128)(2,1)S(1)} %get-tuple-element.68), channel_id=1, source_target_pairs={{0,48},{16,0},{32,16},{48,32},{1,49},{17,1},{33,17},{49,33},{2,50}... | collective-permute-start | bytes 368648 | tf_op jit(solution)/shard_map/ppermute | solution.py:348
  366.9 8.0 %collective-permute-start.28 = (bf16[24,640]{1,0:T(8,128)(2,1)}, bf16[24,640]{1,0:T(8,128)(2,1)S(1)}, u32[]{:S(2)}, u32[]{:S(2)}) collective-permute-start(bf16[24,640]{1,0:T(8,128)(2,1)} %get-tuple-element.88), channel_id=1, source_target_pairs={{0,1},{1,2},{2,3},{3,0},{4,5},{5,6},{6,7},{7,4},{8,9},{9,10},{10,1... | collective-permute-start | bytes 92168 | tf_op jit(solution)/shard_map/ppermute | solution.py:348
  369.4 5.7 %collective-permute-start.29 = (bf16[24,640]{1,0:T(8,128)(2,1)S(1)}, bf16[24,640]{1,0:T(8,128)(2,1)S(1)}, u32[]{:S(2)}, u32[]{:S(2)}) collective-permute-start(bf16[24,640]{1,0:T(8,128)(2,1)S(1)} %get-tuple-element.90), channel_id=1, source_target_pairs={{0,2},{1,3},{2,0},{3,1},{4,6},{5,7},{6,4},{7,5},{8,10},{9,11},{10,... | collective-permute-start | bytes 92168 | tf_op jit(solution)/shard_map/ppermute | solution.py:348
  370.9 6.4 %collective-permute-start.30 = (bf16[24,640]{1,0:T(8,128)(2,1)S(1)}, bf16[24,640]{1,0:T(8,128)(2,1)S(1)}, u32[]{:S(2)}, u32[]{:S(2)}) collective-permute-start(bf16[24,640]{1,0:T(8,128)(2,1)S(1)} %get-tuple-element.89), channel_id=1, source_target_pairs={{0,3},{1,0},{2,1},{3,2},{4,7},{5,4},{6,5},{7,6},{8,11},{9,8},{10,9... | collective-permute-start | bytes 92168 | tf_op jit(solution)/shard_map/ppermute | solution.py:348
  372.4 7.3 %collective-permute-start.37 = (bf16[24,640]{1,0:T(8,128)(2,1)S(1)}, bf16[24,640]{1,0:T(8,128)(2,1)S(1)}, u32[]{:S(2)}, u32[]{:S(2)}) collective-permute-start(bf16[24,640]{1,0:T(8,128)(2,1)S(1)} %get-tuple-element.91), channel_id=1, source_target_pairs={{0,16},{16,32},{32,48},{48,0},{1,17},{17,33},{33,49},{49,1},{2,18}... | collective-permute-start | bytes 92168 | tf_op jit(solution)/shard_map/ppermute | solution.py:348
  374.9 6.4 %collective-permute-start.38 = (bf16[24,640]{1,0:T(8,128)(2,1)S(1)}, bf16[24,640]{1,0:T(8,128)(2,1)S(1)}, u32[]{:S(2)}, u32[]{:S(2)}) collective-permute-start(bf16[24,640]{1,0:T(8,128)(2,1)S(1)} %get-tuple-element.93), channel_id=1, source_target_pairs={{0,32},{16,48},{32,0},{48,16},{1,33},{17,49},{33,1},{49,17},{2,34}... | collective-permute-start | bytes 92168 | tf_op jit(solution)/shard_map/ppermute | solution.py:348
  375.1 7.4 %collective-permute-start.39 = (bf16[24,640]{1,0:T(8,128)(2,1)S(1)}, bf16[24,640]{1,0:T(8,128)(2,1)S(1)}, u32[]{:S(2)}, u32[]{:S(2)}) collective-permute-start(bf16[24,640]{1,0:T(8,128)(2,1)S(1)} %get-tuple-element.92), channel_id=1, source_target_pairs={{0,48},{16,0},{32,16},{48,32},{1,49},{17,1},{33,17},{49,33},{2,50}... | collective-permute-start | bytes 92168 | tf_op jit(solution)/shard_map/ppermute | solution.py:348
  377.4 5.2 %collective-permute-start.46 = (bf16[24,640]{1,0:T(8,128)(2,1)S(1)}, bf16[24,640]{1,0:T(8,128)(2,1)S(1)}, u32[]{:S(2)}, u32[]{:S(2)}) collective-permute-start(bf16[24,640]{1,0:T(8,128)(2,1)S(1)} %get-tuple-element.94), channel_id=1, source_target_pairs={{0,4},{4,8},{8,12},{12,0},{1,5},{5,9},{9,13},{13,1},{2,6},{6,10},{... | collective-permute-start | bytes 92168 | tf_op jit(solution)/shard_map/ppermute | solution.py:348
  384.6 21.9 %collective-permute-start.49 = (f32[24,1920]{1,0:T(8,128)S(1)}, f32[24,1920]{1,0:T(8,128)S(1)}, u32[]{:S(2)}, u32[]{:S(2)}) collective-permute-start(f32[24,1920]{1,0:T(8,128)S(1)} %pad_maximum_fusion.5), channel_id=1, source_target_pairs={{0,64},{64,0},{1,65},{65,1},{2,66},{66,2},{3,67},{67,3},{4,68},{68... | collective-permute-start | bytes 552968 | tf_op jit(solution)/shard_map/ppermute | solution.py:352
  392.0 5.2 %collective-permute-start.10 = (f32[9,1536]{1,0:T(8,128)S(1)}, f32[9,1536]{1,0:T(8,128)S(1)}, u32[]{:S(2)}, u32[]{:S(2)}) collective-permute-start(f32[9,1536]{1,0:T(8,128)S(1)} %maximum_maximum_fusion), channel_id=1, source_target_pairs={{0,48},{16,0},{32,16},{48,32},{1,49},{17,1},{33,17},{49,33},{2,50}... | collective-permute-start | bytes 165896 | tf_op jit(solution)/shard_map/ppermute | solution.py:348
  392.7 5.2 %collective-permute-start.8 = (f32[9,1536]{1,0:T(8,128)S(1)}, f32[9,1536]{1,0:T(8,128)S(1)}, u32[]{:S(2)}, u32[]{:S(2)}) collective-permute-start(f32[9,1536]{1,0:T(8,128)S(1)} %maximum_maximum_fusion), channel_id=1, source_target_pairs={{0,16},{16,32},{32,48},{48,0},{1,17},{17,33},{33,49},{49,1},{2,18}... | collective-permute-start | bytes 165896 | tf_op jit(solution)/shard_map/ppermute | solution.py:348
  393.5 9.2 %collective-permute-start.9 = (f32[9,1536]{1,0:T(8,128)S(1)}, f32[9,1536]{1,0:T(8,128)S(1)}, u32[]{:S(2)}, u32[]{:S(2)}) collective-permute-start(f32[9,1536]{1,0:T(8,128)S(1)} %maximum_maximum_fusion), channel_id=1, source_target_pairs={{0,32},{16,48},{32,0},{48,16},{1,33},{17,49},{33,1},{49,17},{2,34}... | collective-permute-start | bytes 165896 | tf_op jit(solution)/shard_map/ppermute | solution.py:348
  402.7 6.9 %collective-permute-start.11 = (f32[9,1536]{1,0:T(8,128)S(1)}, f32[9,1536]{1,0:T(8,128)S(1)}, u32[]{:S(2)}, u32[]{:S(2)}) collective-permute-start(f32[9,1536]{1,0:T(8,128)S(1)} %add_add_fusion.2), channel_id=1, source_target_pairs={{0,4},{4,8},{8,12},{12,0},{1,5},{5,9},{9,13},{13,1},{2,6},{6,10},{... | collective-permute-start | bytes 165896 | tf_op jit(solution)/shard_map/ppermute | solution.py:348
  402.8 10.3 %collective-permute-start.12 = (f32[9,1536]{1,0:T(8,128)S(1)}, f32[9,1536]{1,0:T(8,128)S(1)}, u32[]{:S(2)}, u32[]{:S(2)}) collective-permute-start(f32[9,1536]{1,0:T(8,128)S(1)} %add_add_fusion.2), channel_id=1, source_target_pairs={{0,8},{4,12},{8,0},{12,4},{1,9},{5,13},{9,1},{13,5},{2,10},{6,14},... | collective-permute-start | bytes 165896 | tf_op jit(solution)/shard_map/ppermute | solution.py:348
  406.5 6.7 %collective-permute-start.13 = (f32[9,1536]{1,0:T(8,128)S(1)}, f32[9,1536]{1,0:T(8,128)S(1)}, u32[]{:S(2)}, u32[]{:S(2)}) collective-permute-start(f32[9,1536]{1,0:T(8,128)S(1)} %add_add_fusion.2), channel_id=1, source_target_pairs={{0,12},{4,0},{8,4},{12,8},{1,13},{5,1},{9,5},{13,9},{2,14},{6,2},{... | collective-permute-start | bytes 165896 | tf_op jit(solution)/shard_map/ppermute | solution.py:348
  439.3 11.8 %collective-permute-start.18 = (bf16[24,1536]{1,0:T(8,128)(2,1)S(1)}, bf16[24,1536]{1,0:T(8,128)(2,1)S(1)}, u32[]{:S(2)}, u32[]{:S(2)}) collective-permute-start(bf16[24,1536]{1,0:T(8,128)(2,1)S(1)} %get-tuple-element.81), channel_id=1, source_target_pairs={{0,1},{1,2},{2,3},{3,0},{4,5},{5,6},{6,7},{7,4},{8,9},{9,10},{10,1... | collective-permute-start | bytes 221192 | tf_op jit(solution)/shard_map/ppermute | solution.py:348
  440.2 12.1 %collective-permute-start.19 = (bf16[24,1536]{1,0:T(8,128)(2,1)S(1)}, bf16[24,1536]{1,0:T(8,128)(2,1)S(1)}, u32[]{:S(2)}, u32[]{:S(2)}) collective-permute-start(bf16[24,1536]{1,0:T(8,128)(2,1)S(1)} %get-tuple-element.82), channel_id=1, source_target_pairs={{0,2},{1,3},{2,0},{3,1},{4,6},{5,7},{6,4},{7,5},{8,10},{9,11},{10,... | collective-permute-start | bytes 221192 | tf_op jit(solution)/shard_map/ppermute | solution.py:348
  443.0 9.4 %collective-permute-start.20 = (bf16[24,1536]{1,0:T(8,128)(2,1)S(1)}, bf16[24,1536]{1,0:T(8,128)(2,1)S(1)}, u32[]{:S(2)}, u32[]{:S(2)}) collective-permute-start(bf16[24,1536]{1,0:T(8,128)(2,1)S(1)} %get-tuple-element.83), channel_id=1, source_target_pairs={{0,3},{1,0},{2,1},{3,2},{4,7},{5,4},{6,5},{7,6},{8,11},{9,8},{10,9... | collective-permute-start | bytes 221192 | tf_op jit(solution)/shard_map/ppermute | solution.py:348
  447.4 8.1 %collective-permute-start.50 = (bf16[48,768]{1,0:T(8,128)(2,1)S(1)}, bf16[48,768]{1,0:T(8,128)(2,1)S(1)}, u32[]{:S(2)}, u32[]{:S(2)}) collective-permute-start(bf16[48,768]{1,0:T(8,128)(2,1)S(1)} %get-tuple-element.76), channel_id=1, source_target_pairs={{0,1},{1,2},{2,3},{3,0},{4,5},{5,6},{6,7},{7,4},{8,9},{9,10},{10,1... | collective-permute-start | bytes 221192 | tf_op jit(solution)/shard_map/ppermute | solution.py:348
  448.7 6.8 %collective-permute-start.51 = (bf16[48,768]{1,0:T(8,128)(2,1)S(1)}, bf16[48,768]{1,0:T(8,128)(2,1)S(1)}, u32[]{:S(2)}, u32[]{:S(2)}) collective-permute-start(bf16[48,768]{1,0:T(8,128)(2,1)S(1)} %get-tuple-element.77), channel_id=1, source_target_pairs={{0,2},{1,3},{2,0},{3,1},{4,6},{5,7},{6,4},{7,5},{8,10},{9,11},{10,... | collective-permute-start | bytes 221192 | tf_op jit(solution)/shard_map/ppermute | solution.py:348
  452.4 6.1 %collective-permute-start.21 = (f32[24,1536]{1,0:T(8,128)S(1)}, f32[24,1536]{1,0:T(8,128)S(1)}, u32[]{:S(2)}, u32[]{:S(2)}) collective-permute-start(f32[24,1536]{1,0:T(8,128)S(1)} %fusion.46), channel_id=1, source_target_pairs={{0,64},{64,0},{1,65},{65,1},{2,66},{66,2},{3,67},{67,3},{4,68},{68... | collective-permute-start | bytes 442376 | tf_op jit(solution)/shard_map/ppermute | solution.py:352
  (81 other events, 1102.0 us)
Sparse Core Ops, SparseCore 0:
  11.4 71.2 all-gather.7
  86.0 69.6 all-gather.3
  158.5 67.6 all-gather.5
  254.0 90.5 reduce-scatter.2
  364.0 82.3 reduce-scatter.4

commit v2 on v1

--- a/solution.py
+++ b/solution.py
@@ -10,6 +10,7 @@
 from jax.sharding import PartitionSpec as P
 
 LEN = 256
+VMEM = 24 * 2**20
 HALF = 128
 HEAD = 64
 GROUP = 8
@@ -149,7 +150,7 @@
 def mix_backward_kernel(
     proj_ref, shared_ref, near_ref, seg_col_ref, seg_row_ref, taps_ref, taps_shared_ref, head_ref,
     ssd_ref, dssd_ref,
-    dproj_ref, drows_ref, drows_shared_ref, dheads_ref,
+    dproj_ref, drows_ref,
     scores, apart, totals, totals_row, steps, b_keep, c_keep, dscores, dtotal, dstep,
 ):
     group = pl.program_id(1)
@@ -234,7 +235,7 @@
     dmixed = wide(dx_parts) * silu_slope(mixed, gate)
     dvalues, rows = convolve_back(dmixed, values, taps_ref[0:4], near)
     dproj_ref[:, pl.ds(pl.multiple_of(group * WIDE, WIDE), WIDE)] = dvalues.astype(bf16)
-    drows_ref[0] = jnp.concatenate(
+    drows_ref[0, :, pl.ds(pl.multiple_of(group * WIDE, WIDE), WIDE)] = jnp.concatenate(
         rows + [wide(skip_parts), jnp.zeros((2, WIDE), f32)], axis=0
     )
 
@@ -251,16 +252,18 @@
         )
         dmixed = jnp.concatenate([db, dc], axis=1) * silu_slope(mixed, gate)
         dvalues, rows = convolve_back(dmixed, values, taps_shared_ref[0:4], near)
-        drows_shared_ref[0] = jnp.concatenate(rows + [jnp.zeros((3, 2 * STATE), f32)], axis=0)
+        at = dproj_ref.shape[1] - 3 * STATE
+        drows_ref[0, :, at : at + 2 * STATE] = jnp.concatenate(
+            rows + [jnp.zeros((3, 2 * STATE), f32)], axis=0
+        )
         raw, step, rate, total = steps_of(shared[:, 2 * STATE :], head_ref[...])
         row, col = positions()
         upper = (row <= col).astype(f32)
         drate = jnp.dot(upper, dtotal[...], precision=highest, preferred_element_type=f32)
         draw = (dstep[...] - drate * head_ref[1:2]) * sigmoid(raw)
-        at = dproj_ref.shape[1] - 3 * STATE
         dproj_ref[:, at : at + 2 * STATE] = dvalues.astype(bf16)
         dproj_ref[:, at + 2 * STATE :] = draw.astype(bf16)
-        dheads_ref[0] = jnp.concatenate(
+        drows_ref[0, :, at + 2 * STATE :] = jnp.concatenate(
             [
                 jnp.sum(draw, axis=0, keepdims=True),
                 jnp.sum(drate * rate, axis=0, keepdims=True),
@@ -303,7 +306,7 @@
         out_specs=pl.BlockSpec((LEN, WIDE), lambda s, g: (s, g)),
         out_shape=jax.ShapeDtypeStruct((rows, columns), f32),
         scratch_shapes=mixer_scratch(groups),
-        compiler_params=pltpu.CompilerParams(vmem_limit_bytes=32 * 2**20),
+        compiler_params=pltpu.CompilerParams(vmem_limit_bytes=VMEM),
         cost_estimate=pl.CostEstimate(flops=10**9, bytes_accessed=8 * 2**20, transcendentals=10**7),
         name="mix_forward",
     )(proj, proj, near, seg_col, seg_row, taps, taps_shared, heads)
@@ -319,15 +322,11 @@
         in_specs=mixer_specs(columns) + [wide, wide],
         out_specs=[
             pl.BlockSpec((LEN, columns + 3 * STATE), lambda s, g: (s, 0)),
-            pl.BlockSpec((1, 8, WIDE), lambda s, g: (s, 0, g)),
-            pl.BlockSpec((1, 8, 2 * STATE), lambda s, g: (s, 0, 0)),
-            pl.BlockSpec((1, 8, STATE), lambda s, g: (s, 0, 0)),
+            pl.BlockSpec((1, 8, columns + 3 * STATE), lambda s, g: (s, 0, 0)),
         ],
         out_shape=[
             jax.ShapeDtypeStruct(proj.shape, bf16),
-            jax.ShapeDtypeStruct((seqs, 8, columns), f32),
-            jax.ShapeDtypeStruct((seqs, 8, 2 * STATE), f32),
-            jax.ShapeDtypeStruct((seqs, 8, STATE), f32),
+            jax.ShapeDtypeStruct((seqs, 8, proj.shape[1]), f32),
         ],
         scratch_shapes=mixer_scratch(groups)
         + [
@@ -337,15 +336,247 @@
             pltpu.VMEM((LEN, STATE), f32),
             pltpu.VMEM((LEN, STATE), f32),
         ],
-        compiler_params=pltpu.CompilerParams(vmem_limit_bytes=40 * 2**20),
+        compiler_params=pltpu.CompilerParams(vmem_limit_bytes=VMEM),
         cost_estimate=pl.CostEstimate(flops=3 * 10**9, bytes_accessed=12 * 2**20, transcendentals=10**7),
         name="mix_backward",
     )(proj, proj, near, seg_col, seg_row, taps, taps_shared, heads, ssd, dssd)
 
 
-def shifted(value, axis, by):
-    size = lax.axis_size(axis)
-    return lax.ppermute(value, axis, [(i, (i + by) % size) for i in range(size)])
+SMALL = 8
+
+
+def two_parts(rows):
+    high = rows.astype(bf16).astype(f32)
+    return [high, rows - high]
+
+
+OVER_TOKENS = (((0,), (0,)), ((), ()))
+
+
+def grad_pieces_kernel(left_ref, right_ref, small_ref, extra_ref, *out_refs):
+    rows = left_ref.shape[1] // SIDE
+    small = jnp.concatenate(two_parts(small_ref[0] + small_ref[1] + extra_ref[...]), axis=0)
+    for k, out_ref in enumerate(out_refs):
+        out_ref[:rows] = lax.dot_general(
+            left_ref[:, k * rows : (k + 1) * rows], right_ref[...], OVER_TOKENS,
+            preferred_element_type=f32,
+        ).astype(out_ref.dtype)
+        out_ref[rows:] = small.astype(out_ref.dtype)
+
+
+def grad_pieces(left, right, small, extra):
+    rows, columns = left.shape[1] // SIDE + 2 * SMALL, right.shape[1]
+    wide = columns // 3
+    return pl.pallas_call(
+        grad_pieces_kernel,
+        grid=(3,),
+        in_specs=[
+            pl.BlockSpec(left.shape, lambda j: (0, 0)),
+            pl.BlockSpec((right.shape[0], wide), lambda j: (0, j)),
+            pl.BlockSpec((2, SMALL, wide), lambda j: (0, 0, j)),
+            pl.BlockSpec((SMALL, wide), lambda j: (0, j)),
+        ],
+        out_specs=[pl.BlockSpec((rows, wide), lambda j: (0, j))] * SIDE,
+        out_shape=[
+            jax.ShapeDtypeStruct((rows, columns), bf16 if k else f32) for k in range(SIDE)
+        ],
+        compiler_params=pltpu.CompilerParams(vmem_limit_bytes=VMEM),
+        cost_estimate=pl.CostEstimate(
+            flops=2 * SIDE * rows * columns * left.shape[0], bytes_accessed=10 * 2**20, transcendentals=0
+        ),
+        name="grad_pieces",
+    )(left, right, small, extra)
+
+
+def tokens_kernel(
+    core_ref, dgate_ref, gate_ref, dproj_ref, reorder_ref, own_mixed_ref, other_mixed_ref, out_ref,
+    *refs,
+):
+    mix_refs = refs[:SIDE]
+    own_ref, other_ref, branch_own_ref, branch_other_ref, total, branch = refs[SIDE:]
+    step = pl.program_id(0)
+    core = core_ref[0]
+    turned = (((1,), (1,)), ((), ()))
+    wide = gate_ref.shape[0]
+    for k, ref in enumerate(mix_refs):
+
+        @pl.when(step == k)
+        def _(k=k, ref=ref):
+            back = lax.dot_general(dproj_ref[...], ref[...], turned, preferred_element_type=f32)
+            back = lax.dot_general(
+                back.astype(bf16), reorder_ref[...], turned, preferred_element_type=f32
+            )
+            if k == 0:
+                total[...] = back
+            else:
+                total[...] += back
+
+    at = pl.ds(pl.multiple_of(step * wide, wide), wide)
+    total[:, at] += lax.dot_general(dgate_ref[...], gate_ref[...], turned, preferred_element_type=f32)
+    mixed = jnp.where(step // (SIDE // 2) == core, own_mixed_ref[...], other_mixed_ref[...])
+    part = jnp.dot(mixed, out_ref[...], preferred_element_type=f32)
+
+    @pl.when(step == 0)
+    def _():
+        branch[...] = part
+
+    @pl.when(step > 0)
+    def _():
+        branch[...] += part
+
+    @pl.when(step == SIDE - 1)
+    def _():
+        own = pl.ds(pl.multiple_of(core * LEN, LEN), LEN)
+        other = pl.ds(pl.multiple_of((1 - core) * LEN, LEN), LEN)
+        own_ref[...] = total[own, :]
+        other_ref[...] = total[other, :].astype(bf16)
+        branch_own_ref[...] = branch[own, :].astype(bf16)
+        branch_other_ref[...] = branch[other, :].astype(bf16)
+
+
+def tokens_parts(core, dgate, w_rest, dproj, reorder, own_mixed, other_mixed, w_out, w_mix):
+    rows, width, half = dproj.shape[0], reorder.shape[0], own_mixed.shape[1]
+    wide = width // SIDE
+    full = lambda array: pl.BlockSpec(array.shape, lambda j: (0, 0))
+    mixed = pl.BlockSpec((rows, 2 * half // SIDE), lambda j: (0, j % (SIDE // 2)))
+    return pl.pallas_call(
+        tokens_kernel,
+        grid=(SIDE,),
+        in_specs=[
+            pl.BlockSpec(memory_space=pltpu.SMEM),
+            full(dgate),
+            pl.BlockSpec((wide, dgate.shape[1]), lambda j: (j, 0)),
+            full(dproj),
+            pl.BlockSpec((width, wide), lambda j: (0, j)),
+            mixed,
+            mixed,
+            pl.BlockSpec((2 * half // SIDE, w_out.shape[1]), lambda j: (j, 0)),
+        ]
+        + [full(piece) for piece in w_mix],
+        out_specs=[pl.BlockSpec((LEN, width), lambda j: (0, 0))] * 2
+        + [pl.BlockSpec((LEN, w_out.shape[1]), lambda j: (0, 0))] * 2,
+        out_shape=[
+            jax.ShapeDtypeStruct((LEN, width), f32),
+            jax.ShapeDtypeStruct((LEN, width), bf16),
+        ]
+        + [jax.ShapeDtypeStruct((LEN, w_out.shape[1]), bf16)] * 2,
+        scratch_shapes=[pltpu.VMEM((rows, width), f32), pltpu.VMEM((rows, w_out.shape[1]), f32)],
+        compiler_params=pltpu.CompilerParams(vmem_limit_bytes=56 * 2**20),
+        cost_estimate=pl.CostEstimate(
+            flops=10**10, bytes_accessed=32 * 2**20, transcendentals=0
+        ),
+        name="tokens_parts",
+    )(core, dgate, w_rest, dproj, reorder, own_mixed, other_mixed, w_out, *w_mix)
+
+
+def fold_kernel(own_ref, one_ref, two_ref, three_ref, extra_ref, out_ref, *send_refs):
+    rows = own_ref.shape[0] // 16 * 16
+    kept = (own_ref.shape[0] - 2 * SMALL) // 16 * 16
+    refs = (own_ref, one_ref, two_ref, three_ref)
+    part = kept // 4
+    small = extra_ref[...]
+    for ref in refs:
+        tail = ref[kept : kept + 2 * SMALL].astype(f32)
+        small = small + tail[:SMALL] + tail[SMALL:]
+    fill = [jnp.zeros((out_ref.shape[0] - part - 2 * SMALL, small.shape[1]), f32)]
+    fill = fill if fill[0].shape[0] else []
+    for k in range(4):
+        total = sum(ref[k * part : (k + 1) * part].astype(f32) for ref in refs)
+        if k == 0:
+            out_ref[...] = jnp.concatenate([total, small, jnp.zeros_like(small)] + fill, axis=0)
+        else:
+            send_refs[k - 1][...] = jnp.concatenate(
+                [total] + two_parts(small) + fill, axis=0
+            ).astype(bf16)
+
+
+def fold(own, received, extra):
+    columns = own.shape[1]
+    kept = (own.shape[0] - 2 * SMALL) // 16 * 16
+    rows = -(-(kept // 4 + 2 * SMALL) // 16) * 16
+    wide = columns // 5
+    block = pl.BlockSpec((own.shape[0], wide), lambda j: (0, j))
+    out = pl.BlockSpec((rows, wide), lambda j: (0, j))
+    return pl.pallas_call(
+        fold_kernel,
+        grid=(5,),
+        in_specs=[block] * 4 + [pl.BlockSpec((SMALL, wide), lambda j: (0, j))],
+        out_specs=[out] * 4,
+        out_shape=[jax.ShapeDtypeStruct((rows, columns), f32)]
+        + [jax.ShapeDtypeStruct((rows, columns), bf16)] * 3,
+        compiler_params=pltpu.CompilerParams(vmem_limit_bytes=VMEM),
+        cost_estimate=pl.CostEstimate(flops=10**7, bytes_accessed=8 * 2**20, transcendentals=0),
+        name="fold",
+    )(own, *received, extra)
+
+
+def owners_kernel(core_ref, own_ref, other_ref, cot_ref, normed_ref, dgate_ref, out_ref):
+    shards, width = out_ref.shape[0], out_ref.shape[2]
+    mine = pl.program_id(0) // (pl.num_programs(0) // 2) == core_ref[0]
+    mixed = jnp.where(mine, own_ref[...], other_ref[...])
+    grad_out = lax.dot_general(
+        mixed, cot_ref[...], OVER_TOKENS, preferred_element_type=f32
+    ).reshape(shards, -1, width)
+    grad_gate = lax.dot_general(
+        normed_ref[...], dgate_ref[...], OVER_TOKENS, preferred_element_type=f32
+    )
+    grad_gate = grad_gate.reshape(shards, -1, 2 * width)
+    out_ref[...] = jnp.concatenate(
+        [grad_out, grad_gate[:, :, :width], grad_gate[:, :, width:]], axis=1
+    ).astype(bf16)
+
+
+def owners_grads(core, own, other, cot, normed, dgate, shards):
+    steps = 4
+    each = shards // steps
+    width = cot.shape[1]
+    rows_out, rows_in = 2 * own.shape[1] // shards, normed.shape[1] // shards
+    mixed = pl.BlockSpec((own.shape[0], each * rows_out), lambda j: (0, j % (steps // 2)))
+    rows = rows_out + 2 * rows_in
+    return pl.pallas_call(
+        owners_kernel,
+        grid=(steps,),
+        in_specs=[
+            pl.BlockSpec(memory_space=pltpu.SMEM),
+            mixed,
+            mixed,
+            pl.BlockSpec(cot.shape, lambda j: (0, 0)),
+            pl.BlockSpec((normed.shape[0], each * rows_in), lambda j: (0, j)),
+            pl.BlockSpec(dgate.shape, lambda j: (0, 0)),
+        ],
+        out_specs=pl.BlockSpec((each, rows, width), lambda j: (j, 0, 0)),
+        out_shape=jax.ShapeDtypeStruct((shards, rows, width), bf16),
+        compiler_params=pltpu.CompilerParams(vmem_limit_bytes=VMEM),
+        cost_estimate=pl.CostEstimate(
+            flops=2 * cot.shape[0] * shards * rows * width, bytes_accessed=16 * 2**20, transcendentals=0
+        ),
+        name="owners_grads",
+    )(core, own, other, cot, normed, dgate)
+
+
+CHIPS = ("z", "y", "x")
+ALL = ("grp",) + CHIPS
+SIDE = 4
+ORDERS = (("x", "y", "z"), ("y", "z", "x"))
+
+
+def place(core, spot):
+    index = core
+    for axis in CHIPS:
+        index = index * SIDE + spot[axis] % SIDE
+    return index
+
+
+def moved(value, phase, by, orders=ORDERS):
+    pairs = []
+    for core in range(2):
+        for z in range(SIDE):
+            for y in range(SIDE):
+                for x in range(SIDE):
+                    spot = dict(z=z, y=y, x=x)
+                    axis = orders[core][phase]
+                    pairs.append((place(core, spot), place(core, {**spot, axis: spot[axis] + by})))
+    return lax.ppermute(value, ALL, pairs)
 
 
 def swapped(value):
@@ -362,22 +593,26 @@
     return lax.dynamic_slice_in_dim(twice, by, value.shape[dim], dim)
 
 
-def summed_over(value, axis):
-    total = value
-    for by in range(1, lax.axis_size(axis)):
-        total = total + shifted(value, axis, by)
-    return total
-
-
-def scattered(pieces, axis):
-    total = pieces[0]
-    for by in range(1, len(pieces)):
-        total = total + shifted(pieces[by].astype(bf16), axis, by).astype(f32)
-    return total
-
-
-def halved(array, size, dim):
-    return lax.dynamic_slice_in_dim(array, lax.axis_index("grp") * size, size, dim)
+def gathered(own, orders):
+    for phase in (2, 1):
+        own = jnp.concatenate([own] + [moved(own, phase, -k, orders) for k in range(1, SIDE)])
+    return [own] + [moved(own, 0, -k, orders) for k in range(1, SIDE)]
+
+
+def row_places(rows, orders):
+    index = lax.iota(jnp.int32, SIDE**3 * rows)
+    steps = (index // (SIDE * SIDE * rows), index // (SIDE * rows) % SIDE, index // rows % SIDE)
+    core = lax.axis_index("grp")
+    places = []
+    for order in orders:
+        spot = {axis: (lax.axis_index(axis) + step) % SIDE for axis, step in zip(order, steps)}
+        places.append(((spot["z"] * SIDE + spot["y"]) * SIDE + spot["x"]) * rows + index % rows)
+    return jnp.where(core == 0, places[0], places[1])
+
+
+def halved(array, size, dim, other=False):
+    core = lax.axis_index("grp")
+    return lax.dynamic_slice_in_dim(array, (1 - core if other else core) * size, size, dim)
 
 
 def times(left, right):
@@ -386,10 +621,6 @@
 
 def times_turned(left, right):
     return lax.dot_general(left, right, (((1,), (1,)), ((), ())), preferred_element_type=f32)
-
-
-CHIPS = ("z", "y", "x")
-ORDERS = (("z", "y", "x"), ("y", "x", "z"), ("x", "z", "y"))
 
 
 def on_device(
@@ -412,22 +643,23 @@
     heads = dt_bias.shape[0] // 2
     bc = conv_bias.shape[0] - inner
     rows_in, rows_out = in_weight.shape[0], out_weight.shape[0]
-
-    w_dt = halved(in_weight[:, inner + inner + bc :], heads, 1)
+    shards = SIDE**3
+
     own_mix = jnp.concatenate(
         [
             halved(in_weight[:, inner : 2 * inner], half, 1),
             in_weight[:, 2 * inner : 2 * inner + bc],
-            w_dt,
+            halved(in_weight[:, inner + inner + bc :], heads, 1),
             jnp.zeros((rows_in, STATE - heads), bf16),
         ],
         axis=1,
     )
-    own_gate = halved(in_weight[:, :inner], half, 1)
     own_out = halved(out_weight, width // 2, 1)
-    w_mix = lax.all_gather(own_mix, CHIPS, axis=0, tiled=True)
-    w_gate = lax.all_gather(own_gate, CHIPS, axis=0, tiled=True)
-    w_out = lax.all_gather(own_out, CHIPS, axis=0, tiled=True)
+    own_rest = jnp.concatenate(
+        [halved(in_weight[:, :inner], half, 1), own_out[:rows_in], own_out[rows_in:]], axis=1
+    )
+    w_rest = lax.all_gather(own_rest, CHIPS, axis=0, tiled=True)
+    w_mix = gathered(own_mix, ORDERS)
 
     residual = tokens.astype(f32)
     scale = lax.rsqrt(jnp.mean(residual * residual, axis=-1, keepdims=True) + NORM_EPS)
@@ -449,7 +681,8 @@
             halved(conv_weight[:, :inner], half, 1),
             halved(conv_bias[None, :inner], half, 1),
             jnp.repeat(halved(skip_d, heads, 0), HEAD)[None],
-            jnp.zeros((2, half), f32),
+            halved(gnorm_gain[None], half, 1),
+            jnp.zeros((1, half), f32),
         ]
     )
     taps_shared = jnp.concatenate(
@@ -459,24 +692,34 @@
     head_rows = jnp.pad(head_rows, ((0, 6), (0, STATE - heads)))
     gain = halved(gnorm_gain, half, 0)
 
-    turned_low = normed.T.reshape(4, 4, 4, rows_in, -1)
-    for dim, axis in enumerate(CHIPS):
-        turned_low = turned(turned_low, dim, lax.axis_index(axis))
-    leaving = []
-    for order in ORDERS:
-        dims = tuple(CHIPS.index(axis) for axis in order)
-        leaving.append(turned_low.transpose(dims + (3, 4)).reshape(4, 16 * rows_in, -1))
-
-    proj = times(normed, w_mix)
+    places = row_places(rows_in, ORDERS)
+    reorder = (lax.iota(jnp.int32, width)[:, None] == places[None, :]).astype(bf16)
+    normed_moved = times(normed, reorder).astype(bf16)
+    cot_half = halved(cot, width // 2, 1)
+
+    core = lax.axis_index("grp")
+    which = core.astype(jnp.int32)[None]
+    quarter = width // SIDE
+    proj = sum(
+        times(normed_moved[:, k * quarter : (k + 1) * quarter], w_mix[k]) for k in range(SIDE)
+    )
     sides = (near, seg_col, seg_row, taps, taps_shared, head_rows)
     ssd = mix_forward(proj, *sides)
-    gate_part = times(normed, w_gate)
-    cot_half = halved(cot, width // 2, 1)
+    ssd, w_rest, reorder, cot_half, normed = lax.optimization_barrier(
+        (ssd, w_rest, reorder, cot_half, normed)
+    )
+    w_out = jnp.stack(
+        [
+            w_rest[:, half : half + width // 2].reshape(shards, rows_in, -1),
+            w_rest[:, half + width // 2 :].reshape(shards, rows_in, -1),
+        ],
+        axis=1,
+    ).reshape(inner, -1)
     mixer_parts = times_turned(cot_half, w_out).astype(bf16)
-    core = lax.axis_index("grp")
     grad_mixer = halved(mixer_parts, half, 1).astype(f32) + swapped(
-        lax.dynamic_slice_in_dim(mixer_parts, (1 - core) * half, half, 1)
+        halved(mixer_parts, half, 1, other=True)
     ).astype(f32)
+    gate_part = times(normed, w_rest[:, :half])
     opened = sigmoid(gate_part)
     gate = gate_part * opened
     gated = ssd * gate
@@ -485,70 +728,68 @@
     sums = sums + swapped(sums)
     gscale = lax.rsqrt(sums[0] / inner + NORM_EPS)[:, None]
     pull = gscale * gscale * gscale * (sums[1] / inner)[:, None]
+    dgated = gscale * weighted - gated * pull
     mixer_low = (gated * gscale * gain).astype(bf16)
-    dgated = gscale * weighted - gated * pull
     grad_gain = jnp.sum(grad_mixer * gated * gscale, axis=0)
     dgate_low = (dgated * ssd * silu_slope(gate_part, opened)).astype(bf16)
     dssd = (dgated * gate).astype(bf16)
     mixer_other = swapped(mixer_low)
-    mixer_all = in_order(mixer_low, mixer_other, axis=1)
-
-    out_grad = lax.dot_general(
-        mixer_all, cot_half, (((0,), (0,)), ((), ())), preferred_element_type=f32
-    ).astype(bf16)
-    gate_grad = times(normed.T, dgate_low).astype(bf16)
-    out_share = lax.psum_scatter(out_grad, ("z", "y"), scatter_dimension=0, tiled=True)
-    gate_share = lax.psum_scatter(gate_grad, ("z", "y"), scatter_dimension=0, tiled=True)
-
-    dproj, drows, drows_shared, dheads = mix_backward(proj, *sides, ssd, dssd)
-    mix_shares = []
-    wide = dproj.shape[1] // 3
-    for stream, order in enumerate(ORDERS):
-        columns = dproj[:, stream * wide : (stream + 1) * wide]
-        pieces = [times(leaving[stream][k], columns) for k in range(4)]
-        share = scattered(pieces, order[0])
-        share = scattered(list(share.reshape(4, 4 * rows_in, wide)), order[1])
-        share = scattered(list(share.reshape(4, rows_in, wide)), order[2])
-        mix_shares.append(share)
-    mix_share = jnp.concatenate(mix_shares, axis=1)
-
-    out_turned = turned(out_share.reshape(4, rows_out, -1), 0, lax.axis_index("x"))
-    out_total = scattered([out_turned[0].astype(f32)] + list(out_turned[1:]), "x")
-    gate_turned = turned(gate_share.reshape(4, rows_in, -1), 0, lax.axis_index("x"))
-    gate_total = scattered([gate_turned[0].astype(f32)] + list(gate_turned[1:]), "x")
-
-    out_part = times(mixer_all, w_out)
-    out_own = halved(out_part, LEN, 0).astype(bf16)
-    out_other = swapped(lax.dynamic_slice_in_dim(out_part, (1 - core) * LEN, LEN, 0).astype(bf16))
-    branch = in_order(out_own, out_other, axis=1)
+
+    rest_grad = owners_grads(which, mixer_low, mixer_other, cot_half, normed, dgate_low, shards)
+    rest_rows = rest_grad.shape[1]
+    gain_row = jnp.zeros((SMALL, proj.shape[1]), f32).at[6, :half].set(grad_gain)
+    rest_grad, dssd, gain_row = lax.optimization_barrier((rest_grad, dssd, gain_row))
+    rest_share = lax.psum_scatter(
+        rest_grad.reshape(shards * rest_rows, -1), ("z", "y"), scatter_dimension=0, tiled=True
+    )
+
+    dproj, drows = mix_backward(proj, *sides, ssd, dssd)
+    own, *gone = grad_pieces(normed_moved, dproj, drows, gain_row)
+    dproj, *gone = lax.optimization_barrier((dproj, *gone))
+    received = [moved(gone[k - 1], 0, k) for k in range(1, SIDE)]
+
+    parts = tokens_parts(
+        which, dgate_low, w_rest, dproj, reorder, mixer_low, mixer_other, w_out, w_mix
+    )
+    nothing = jnp.zeros((SMALL, dproj.shape[1]), f32)
+    *received, nothing, parts = lax.optimization_barrier((*received, nothing, parts))
+    own, *gone = fold(own, received, nothing)
+    parts, *gone = lax.optimization_barrier((parts, *gone))
+    received = [moved(gone[k - 1], 1, k) for k in range(1, SIDE)]
+    normed_own, normed_other, branch_own, branch_other = parts
+    branch = in_order(branch_own, swapped(branch_other), axis=1)
     out_tokens = (residual + branch.astype(f32)).astype(bf16)
-
-    normed_part = times_turned(dproj, w_mix) + times_turned(dgate_low, w_gate)
-    grad_normed = halved(normed_part, LEN, 0) + swapped(
-        lax.dynamic_slice_in_dim(normed_part, (1 - core) * LEN, LEN, 0).astype(bf16)
-    ).astype(f32)
+    grad_normed = normed_own + swapped(normed_other).astype(f32)
     q = grad_normed * norm_gain
     grad_tokens = cotangent.astype(f32) + scale * (
         q - unit * jnp.mean(q * unit, axis=-1, keepdims=True)
     )
-    grad_norm_gain = jnp.sum(grad_normed * unit, axis=0)
-
-    drows, drows_shared, dheads = drows.sum(0), drows_shared.sum(0), dheads.sum(0)
-    small = jnp.concatenate(
-        [
-            drows[:6],
-            grad_gain[None],
-            grad_norm_gain[None],
-            jnp.concatenate([drows_shared[:5].reshape(1, -1), dheads[:2].reshape(1, -1)], axis=1),
-        ]
-    )
-    for axis in CHIPS:
-        small = summed_over(small, axis)
+    grad_norm_gain = jnp.sum(grad_normed * unit, axis=0)[None]
+    for phase in range(2):
+        grad_norm_gain = grad_norm_gain + sum(
+            moved(grad_norm_gain, phase, k) for k in range(1, SIDE)
+        )
+    extra = nothing.at[SMALL - 1, :width].set(grad_norm_gain[0])
+    own, *gone = fold(own, received, extra)
+
+    rest_turned = turned(rest_share.reshape(SIDE, rest_rows, -1), 0, lax.axis_index("x"))
+    rest_turned, *gone = lax.optimization_barrier((rest_turned, *gone))
+    mix_total = own + sum(moved(gone[k - 1], 2, k).astype(f32) for k in range(1, SIDE))
+    mix_share = mix_total[:rows_in]
+    small = mix_total[rows_in : rows_in + SMALL] + mix_total[rows_in + SMALL : rows_in + 2 * SMALL]
+    rest_total = rest_turned[0].astype(f32) + sum(
+        lax.ppermute(rest_turned[k], "x", [(i, (i + k) % SIDE) for i in range(SIDE)]).astype(f32)
+        for k in range(1, SIDE)
+    )
 
     small_other = swapped(small)
-    mix_other, gate_other, out_other = swapped(mix_share), swapped(gate_total), swapped(out_total)
+    mix_other, rest_other = swapped(mix_share), swapped(rest_total)
     bc_sum = (mix_share + mix_other)[:, half : half + bc]
     dt_at = slice(half + bc, half + bc + heads)
+    gate_total, gate_other = (
+        jnp.concatenate([rest[rows_out : rows_out + rows_in], rest[rows_out + rows_in :]], axis=1)
+        for rest in (rest_total, rest_other)
+    )
     grad_in_weight = jnp.concatenate(
         [
             in_order(gate_total, gate_other, axis=1),
@@ -558,19 +799,15 @@
         ],
         axis=1,
     )
-    grad_out_weight = in_order(out_total, out_other, axis=1)
-    both = in_order(small[:7], small_other[:7], axis=1)
-    shared_sum = (small + small_other)[7:]
-    shared_rows = shared_sum[1, : 5 * bc].reshape(5, bc)
-    head_sums = in_order(
-        small[8, 5 * bc :].reshape(2, STATE)[:, :heads],
-        small_other[8, 5 * bc :].reshape(2, STATE)[:, :heads],
-        axis=1,
-    )
+    grad_out_weight = in_order(rest_total[:rows_out], rest_other[:rows_out], axis=1)
+    both = in_order(small[:, :half], small_other[:, :half], axis=1)
+    summed = small + small_other
+    shared_rows = summed[:, half : half + bc]
+    head_sums = in_order(small[:, dt_at], small_other[:, dt_at], axis=1)
     return (
         out_tokens,
         grad_tokens,
-        shared_sum[0],
+        summed[SMALL - 1, :width],
         grad_in_weight,
         jnp.concatenate([both[:4], shared_rows[:4]], axis=1),
         jnp.concatenate([both[4], shared_rows[4]]),
@@ -583,8 +820,8 @@
 
 
 def solution(mesh):
-    chips = Mesh(mesh.devices.reshape(2, 4, 4, 4), ("grp",) + CHIPS)
-    rows = P(("grp",) + CHIPS, None)
+    chips = Mesh(mesh.devices.reshape(2, SIDE, SIDE, SIDE), ALL)
+    rows = P(ALL, None)
     owned = P(CHIPS, None)
     return jax.shard_map(
         on_device,

time: 476 us -> 317 us (0.67)
  waiting for transfers between devices: 229 us -> 106 us
  Pallas kernels: 27.9 us -> 66.3 us
  matrix products: 52.6 us -> 15.3 us
  starting transfers between devices: 77.6 us -> 52.5 us
  other arithmetic: 32.2 us -> 26.8 us
    all_gather x3 -> x1, waiting for transfers between devices: 176 us -> 23.7 us  [on_device(): w_rest = lax.all_gather(own_rest, CHIPS, axis=0, tiled=True)]
    pallas_call x0 -> x5, Pallas kernels: none -> 38.2 us  [the longest x1 23.6 us: tokens_parts(): pl.pallas_call(tokens_kernel, grid=(SIDE,), in_specs=[pl.BlockSpec(memory...]
    ppermute x42 -> x27, waiting for transfers between devices: 46 us -> 74.8 us  [the longest x24 74.8 us: moved(): return lax.ppermute(value, ALL, pairs)]
    dot_general x16 -> x6, matrix products: 34.7 us -> 12.5 us  [times(): return jnp.dot(left, right, preferred_element_type=f32)]
    ppermute x42 -> x27, starting transfers between devices: 53.5 us -> 39.1 us  [the longest x24 34.3 us: moved(): return lax.ppermute(value, ALL, pairs)]
    dot_general x3 -> x1, matrix products: 13.5 us -> 2.86 us  [times_turned(): lax.dot_general(left, right, (((1,), (1,)), ((), ())), preferred_element_...]
    ppermute x12 -> x11, starting transfers between devices: 23.9 us -> 13.4 us  [swapped(): return lax.ppermute(value, 'grp', [(0, 1), (1, 0)])]
    unnamed x139 -> x91, local copies, waits for them, and re-layouts: 12.9 us -> 19 us
  transfers between devices with their start and end apart: 59 -> 40, of which waited for: 23 -> 18; matrix products, arithmetic and copies ran while one was open for 18% -> 12% of each run, Pallas kernels for 6% -> 19%
where the time goes in v2:
time: 317 us; the launch traced here: 311 us
  waiting for transfers between devices  106 us (33%)
  Pallas kernels  66.3 us (21%)
  starting transfers between devices  52.5 us (17%)
  local copies, waits for them, and re-layouts  28.8 us (9%)
  other arithmetic  26.8 us (8%)
  matrix products  15.3 us (5%)
  between operations  15.1 us (5%)
    ppermute x24, waiting for transfers between devices, moved(): return lax.ppermute(value, ALL, pairs)  74.8 us
    ppermute x24, starting transfers between devices, moved(): return lax.ppermute(value, ALL, pairs)  34.3 us
    all_gather x1, waiting for transfers between devices, on_device(): w_rest = lax.all_gather(own_rest, CHIPS, axis=0, tiled=True)  23.7 us
    pallas_call x1, Pallas kernels, tokens_parts(): pl.pallas_call(tokens_kernel, grid=(SIDE,), in_specs=[pl.BlockSpec(memory...  23.6 us
    unnamed x91, local copies, waits for them, and re-layouts  19 us
    pallas_call x1, Pallas kernels, mix_backward(): pl.pallas_call(mix_backward_kernel, grid=(seqs, groups), in_specs=mixer_s...  19 us
    ppermute x11, starting transfers between devices, swapped(): return lax.ppermute(value, 'grp', [(0, 1), (1, 0)])  13.4 us
    dot_general x6, matrix products, times(): return jnp.dot(left, right, preferred_element_type=f32)  12.5 us
  transfers between devices with their start and end apart: 40, of which 18 were waited for; matrix products, arithmetic and copies ran while one was open for 12% of the time, Pallas kernels for 19%

profile of v2, /device:TPU:1, one launch (start us, length us, event | category | flops | bytes accessed | tf_op | source)
XLA Modules:
  0.0 311.1 jit_solution(7749973301778777649)
XLA Ops:
  10.8 3.3 %collective-permute-start.1 = (bf16[24,1920]{1,0:T(8,128)(2,1)S(1)}, bf16[24,1920]{1,0:T(8,128)(2,1)S(1)}, u32[]{:S(2)}, u32[]{:S(2)}) collective-permute-start(bf16[24,1920]{1,0:T(8,128)(2,1)S(1)} %concatenate.77), channel_id=1, source_target_pairs={{0,48},{1,49},{2,50},{3,51},{4,52},{5,53},{6,54},{7,55},{8,56},{9,... | collective-permute-start | bytes 276488 | tf_op jit(solution)/shard_map/ppermute | solution.py:579
  15.8 2.4 collective-permute-start
  19.3 4.2 %fusion.reorder_ref = bf16[1536,1536]{1,0:T(8,128)(2,1)} fusion(s32[1536]{0:T(1024)S(1)} %fusion.53), kind=kLoop, calls=%fused_computation.1 | loop fusion | flops 4718592 | bytes 4724736 | tf_op jit(solution)/shard_map/convert_element_type | solution.py:696
  26.2 1.8 collective-permute-start.4
  27.9 2.0 collective-permute-start.5
  31.9 2.1 collective-permute-done.4
  34.8 1.9 collective-permute-done.5
  37.4 3.5 %collective-permute-done.6 = bf16[96,1920]{1,0:T(8,128)(2,1)S(1)} collective-permute-done((bf16[96,1920]{1,0:T(8,128)(2,1)S(1)}, bf16[96,1920]{1,0:T(8,128)(2,1)S(1)}, u32[]{:S(2)}, u32[]{:S(2)}) %collective-permute-start.6) | collective-permute-done | bytes 368672 | tf_op jit(solution)/shard_map/ppermute | solution.py:579
  41.7 2.7 collective-permute-start.7
  45.5 1.7 broadcast_select_fusion
  47.3 2.7 fusion.6.left_ref
  52.2 2.6 fusion.31
  54.8 28.0 %collective-permute-done.7.refs_1_ = bf16[384,1920]{1,0:T(8,128)(2,1)S(1)} collective-permute-done((bf16[384,1920]{1,0:T(8,128)(2,1)}, bf16[384,1920]{1,0:T(8,128)(2,1)S(1)}, u32[]{:S(2)}, u32[]{:S(2)}) %collective-permute-start.7) | collective-permute-done | bytes 1474592 | tf_op jit(solution)/shard_map/ppermute | solution.py:579
  85.3 1.4 collective-permute-done.9.refs_3_
  88.0 9.2 %mix_forward.1.ssd_ref = f32[512,1536]{1,0:T(8,128)S(1)} custom-call(f32[512,1920]{1,0:T(8,128)S(1)} %add_add_fusion.proj_ref.shared_ref, f32[512,1920]{1,0:T(8,128)S(1)} %add_add_fusion.proj_ref.shared_ref, f32[512,8]{1,0:T(8,128)S(1)} %copy.36.near_ref, f32[512,1]{1,0:T(8,128)S(1)} %bitcast.65, f32[2,1,256]{2,1,0:T(1,128)S(1)} %add_convert_fusion.seg_row_ref, ...), custom_call_target="tpu_custom_call" | custom-call | flops 1000000000 | bytes 8388608 | tf_op jit(solution)/shard_map/mix_forward/pallas_call | solution.py:302
  97.2 1.8 copy-done.1
  99.0 23.7 %all-gather.2.cloned.1.call-done.gate_ref = bf16[1536,3072]{1,0:T(8,128)(2,1)} async-done(((bf16[24,3072]{1,0:T(8,128)(2,1)}), bf16[1536,3072]{1,0:T(8,128)(2,1)}) %all-gather.2.cloned.1.call-update) | async-done | bytes 9437200 | tf_op jit(solution)/shard_map/all_gather | solution.py:661
  122.8 2.7 fusion.92
  126.6 2.9 convolution_convert_fusion
  130.8 3.0 collective-permute-done.12
  133.9 3.6 %multiply_reduce_fusion.2 = (f32[512]{0:T(512)S(1)}, f32[512]{0:T(512)S(1)}, f32[512,1536]{1,0:T(8,128)S(1)}) fusion(f32[512,1536]{1,0:T(8,128)S(1)} %mix_forward.1.ssd_ref, f32[1536]{0:T(1024)S(1)} %dynamic-slice.22, bf16[512,1536]{1,0:T(8,128)(2,1)S(1)} %collective-permute-done.12, bf16[512,3072]{1,0:T(8,128)(2,1)S(1)} %convolution_convert_fusion, ...), kind=kOutput, calls=%fused_computation.16 | convolution fusion | flops 2426141696 | bytes 15740932 | tf_op jit(solution)/shard_map/dot_general | solution.py:619
  138.8 4.2 %multiply_convert_fusion = (bf16[512,1536]{1,0:T(8,128)(2,1)}, bf16[512,1536]{1,0:T(8,128)(2,1)S(1)}, f32[1536]{0:T(1024)S(1)}, bf16[512,1536]{1,0:T(8,128)(2,1)S(1)}) fusion(f32[512,1536]{1,0:T(8,128)S(1)} %get-tuple-element.183, f32[512]{0:T(512)S(1)} %fusion.85, bf16[512,1536]{1,0:T(8,128)(2,1)S(1)} %collective-permute-done.12, f32[512]{0:T(512)S(1)} %bitcast.79, ...), kind=kLoop, calls=%fused_computation.10 | loop fusion | flops 21232128 | bytes 14172164 | tf_op jit(solution)/shard_map/convert_element_type | solution.py:735
  143.3 3.1 collective-permute-done.14.other_ref.other_mixed_ref
  146.4 6.4 %owners_grads.1 = bf16[64,96,768]{2,1,0:T(8,128)(2,1)S(1)} custom-call(s32[1]{0:T(128)} %bitcast.5.core_ref, bf16[512,1536]{1,0:T(8,128)(2,1)S(1)} %get-tuple-element.142.own_ref.own_mixed_ref, bf16[512,1536]{1,0:T(8,128)(2,1)S(1)} %collective-permute-done.14.other_ref.other_mixed_ref, bf16[512,768]{1,0:T(8,128)(2,1)S(1)} %copy-done.11, ...), custom_call_target="tpu_custom_call" | custom-call | flops 4831838208 | bytes 16777216 | tf_op jit(solution)/shard_map/owners_grads/pallas_call | solution.py:536
  152.9 3.6 %copy-done = bf16[64,96,768]{2,1,0:T(8,128)(2,1)} copy-done((bf16[64,96,768]{2,1,0:T(8,128)(2,1)}, bf16[64,96,768]{2,1,0:T(8,128)(2,1)S(1)}, u32[]{:S(2)}) %copy-start) | copy-done | bytes 9437208
  156.5 2.1 copy-done.2
  158.6 1.4 copy-done.8
  160.9 19.0 %mix_backward.1 = (bf16[512,1920]{1,0:T(8,128)(2,1)S(1)}, f32[2,8,1920]{2,1,0:T(8,128)S(1)}) custom-call(f32[512,1920]{1,0:T(8,128)S(1)} %copy-done.2, f32[512,1920]{1,0:T(8,128)S(1)} %copy-done.2, f32[512,8]{1,0:T(8,128)S(1)} %copy.36.near_ref, f32[512,1]{1,0:T(8,128)S(1)} %bitcast.66, f32[2,1,256]{2,1,0:T(1,128)S(1)} %add_convert_fusion.seg_row_ref, ...), custom_call_target="tpu_custom_call" | custom-call | flops 3000000000 | bytes 12582912 | tf_op jit(solution)/shard_map/mix_backward/pallas_call | solution.py:319
  179.9 5.9 %grad_pieces.1 = (f32[400,1920]{1,0:T(8,128)S(1)}, bf16[400,1920]{1,0:T(8,128)(2,1)}, bf16[400,1920]{1,0:T(8,128)(2,1)}, bf16[400,1920]{1,0:T(8,128)(2,1)}) custom-call(bf16[512,1536]{1,0:T(8,128)(2,1)S(1)} %copy-done.4, bf16[512,1920]{1,0:T(8,128)(2,1)S(1)} %get-tuple-element.98.right_ref.dproj_ref, f32[2,8,1920]{2,1,0:T(8,128)S(1)} %get-tuple-element.90.small_ref, ...), custom_call_target="tpu_custom_call" | custom-call | flops 3145728000 | bytes 10485760 | tf_op jit(solution)/shard_map/grad_pieces/pallas_call | solution.py:370
  187.0 2.4 collective-permute-start.16
  190.8 23.6 %tokens_parts.1 = (f32[256,1536]{1,0:T(8,128)}, bf16[256,1536]{1,0:T(8,128)(2,1)}, bf16[256,768]{1,0:T(8,128)(2,1)}, bf16[256,768]{1,0:T(8,128)(2,1)}) custom-call(s32[1]{0:T(128)} %bitcast.5.core_ref, bf16[512,1536]{1,0:T(8,128)(2,1)} %copy-done.6, bf16[1536,3072]{1,0:T(8,128)(2,1)} %all-gather.2.cloned.1.call-done.gate_ref, bf16[512,1920]{1,0:T(8,128)(2,1)} %copy-done.17, ...), custom_call_target="tpu_custom_call" | custom-call | flops 10000000000 | bytes 33554432 | tf_op jit(solution)/shard_map/tokens_parts/pallas_call | solution.py:442
  214.4 1.9 collective-permute-done.15.one_ref
  216.3 27.1 %collective-permute-done.16.two_ref = bf16[400,1920]{1,0:T(8,128)(2,1)S(1)} collective-permute-done((bf16[400,1920]{1,0:T(8,128)(2,1)}, bf16[400,1920]{1,0:T(8,128)(2,1)S(1)}, u32[]{:S(2)}, u32[]{:S(2)}) %collective-permute-start.16) | collective-permute-done | bytes 1536032 | tf_op jit(solution)/shard_map/ppermute | solution.py:579
  243.4 1.7 fold.2
  249.0 2.3 collective-permute-start.21
  252.3 2.3 fusion.18
  254.9 2.6 collective-permute-start.24
  259.2 1.4 collective-permute-done.25
  260.7 2.1 collective-permute-start.27
  263.6 1.4 collective-permute-done.26
  264.9 4.6 %collective-permute-start.22 = (bf16[112,1920]{1,0:T(8,128)(2,1)S(1)}, bf16[112,1920]{1,0:T(8,128)(2,1)S(1)}, u32[]{:S(2)}, u32[]{:S(2)}) collective-permute-start(bf16[112,1920]{1,0:T(8,128)(2,1)S(1)} %get-tuple-element.123), channel_id=1, source_target_pairs={{0,12},{1,13},{2,14},{3,15},{4,0},{5,1},{6,2},{7,3},{8,4},{9,5},{1... | collective-permute-start | bytes 1290248 | tf_op jit(solution)/shard_map/ppermute | solution.py:579
  270.0 5.0 %collective-permute-done.22.three_ref = bf16[112,1920]{1,0:T(8,128)(2,1)S(1)} collective-permute-done((bf16[112,1920]{1,0:T(8,128)(2,1)S(1)}, bf16[112,1920]{1,0:T(8,128)(2,1)S(1)}, u32[]{:S(2)}, u32[]{:S(2)}) %collective-permute-start.22) | collective-permute-done | bytes 430112 | tf_op jit(solution)/shard_map/ppermute | solution.py:579
  275.7 1.4 fusion.22
  278.4 2.7 collective-permute-start.34
  282.0 3.8 %fusion.17 = (f32[256,1536]{1,0:T(8,128)}, bf16[256,1536]{1,0:T(8,128)(2,1)}) fusion(bf16[256,1536]{1,0:T(8,128)(2,1)S(1)} %copy-done.19, bf16[256,1536]{1,0:T(8,128)(2,1)} %param.27, f32[256]{0:T(256)S(1)} %broadcast_multiply_fusion, f32[1536]{0:T(1024)S(1)} %copy-done.31, f32[256]{0:T(256)S(1)} %add_rsqrt_fusion, f32[256,1536]{1,0:T(8,128)} %get-tuple-element.118, ...), kind=kLoop, calls=%fused_computation.33 | loop fusion | flops 6291456 | bytes 7086080 | tf_op jit(solution)/shard_map/add | solution.py:764
  287.0 1.8 collective-permute-start.31
  288.8 4.3 %collective-permute-start.36 = (f32[96,768]{1,0:T(8,128)S(1)}, f32[96,768]{1,0:T(8,128)S(1)}, u32[]{:S(2)}, u32[]{:S(2)}) collective-permute-start(f32[96,768]{1,0:T(8,128)S(1)} %convert_add_fusion.3), channel_id=1, source_target_pairs={{0,64},{64,0},{1,65},{65,1},{2,66},{66,2},{3,67},{67,3},{4,68},{68... | collective-permute-start | bytes 884744 | tf_op jit(solution)/shard_map/ppermute | solution.py:583
  294.1 3.5 %collective-permute-start.32 = (f32[8,1920]{1,0:T(8,128)S(1)}, f32[8,1920]{1,0:T(8,128)S(1)}, u32[]{:S(2)}, u32[]{:S(2)}) collective-permute-start(f32[8,1920]{1,0:T(8,128)S(1)} %slice_add_fusion), channel_id=1, source_target_pairs={{0,64},{64,0},{1,65},{65,1},{2,66},{66,2},{3,67},{67,3},{4,68},{68... | collective-permute-start | bytes 184328 | tf_op jit(solution)/shard_map/ppermute | solution.py:583
  (245 shorter events, 47.3 us)
Async XLA Ops:
  7.2 115.6 %all-gather.2.cloned.1.call-start = ((), (), s32[]{:S(2)}) async-start(), calls=%async_computation.1 | async-start | bytes 9584640 | tf_op jit(solution)/shard_map/all_gather | solution.py:661
  9.2 9.1 %copy-start.33 = (s32[1,256]{1,0:T(1,128)S(1)}, s32[1,256]{1,0:T(1,128)}, u32[]{:S(2)}) copy-start(s32[1,256]{1,0:T(1,128)} %param.17) | copy-start | bytes 3076
  9.8 8.8 %slice-start.4 = ((f32[4,3328]{1,0:T(4,128)}), f32[4,3072]{1,0:T(4,128)S(1)}, s32[]{:S(2)}) async-start(f32[4,3328]{1,0:T(4,128)} %param.20), calls=%async_computation.7 | async-start | bytes 98304 | tf_op jit(solution)/shard_map/slice | solution.py:681
  9.9 265.8 %reduce-scatter.2.cloned.1.call-start = ((), (), s32[]{:S(2)}) async-start(), calls=%async_computation.2 | async-start | bytes 10027008 | tf_op jit(solution)/shard_map/reduce_scatter | solution.py:742
  10.8 15.3 %collective-permute-start.1 = (bf16[24,1920]{1,0:T(8,128)(2,1)S(1)}, bf16[24,1920]{1,0:T(8,128)(2,1)S(1)}, u32[]{:S(2)}, u32[]{:S(2)}) collective-permute-start(bf16[24,1920]{1,0:T(8,128)(2,1)S(1)} %concatenate.77), channel_id=1, source_target_pairs={{0,48},{1,49},{2,50},{3,51},{4,52},{5,53},{6,54},{7,55},{8,56},{9,... | collective-permute-start | bytes 276488 | tf_op jit(solution)/shard_map/ppermute | solution.py:579
  14.1 12.0 %collective-permute-start.2 = (bf16[24,1920]{1,0:T(8,128)(2,1)S(1)}, bf16[24,1920]{1,0:T(8,128)(2,1)S(1)}, u32[]{:S(2)}, u32[]{:S(2)}) collective-permute-start(bf16[24,1920]{1,0:T(8,128)(2,1)S(1)} %concatenate.77), channel_id=1, source_target_pairs={{0,32},{1,33},{2,34},{3,35},{4,36},{5,37},{6,38},{7,39},{8,40},{9,... | collective-permute-start | bytes 276488 | tf_op jit(solution)/shard_map/ppermute | solution.py:579
  14.7 11.5 %collective-permute-start.3 = (bf16[24,1920]{1,0:T(8,128)(2,1)S(1)}, bf16[24,1920]{1,0:T(8,128)(2,1)S(1)}, u32[]{:S(2)}, u32[]{:S(2)}) collective-permute-start(bf16[24,1920]{1,0:T(8,128)(2,1)S(1)} %concatenate.77), channel_id=1, source_target_pairs={{0,16},{1,17},{2,18},{3,19},{4,20},{5,21},{6,22},{7,23},{8,24},{9,... | collective-permute-start | bytes 276488 | tf_op jit(solution)/shard_map/ppermute | solution.py:579
  15.8 29.8 %collective-permute-start = (bf16[256,1536]{1,0:T(8,128)(2,1)S(1)}, bf16[256,1536]{1,0:T(8,128)(2,1)}, u32[]{:S(2)}, u32[]{:S(2)}) collective-permute-start(bf16[256,1536]{1,0:T(8,128)(2,1)S(1)} %fusion.13), channel_id=1, source_target_pairs={{0,64},{64,0},{1,65},{65,1},{2,66},{66,2},{3,67},{67,3},{4,68},{68... | collective-permute-start | bytes 2359304 | tf_op jit(solution)/shard_map/ppermute | solution.py:583
  18.2 5.8 %collective-permute-start.10 = (s32[1,256]{1,0:T(1,128)S(1)}, s32[1,256]{1,0:T(1,128)S(1)}, u32[]{:S(2)}, u32[]{:S(2)}) collective-permute-start(s32[1,256]{1,0:T(1,128)S(1)} %copy-done.33), channel_id=1, source_target_pairs={{0,64},{64,0},{1,65},{65,1},{2,66},{66,2},{3,67},{67,3},{4,68},{68... | collective-permute-start | bytes 3080 | tf_op jit(solution)/shard_map/ppermute | solution.py:583
  24.1 21.5 %collective-permute-start.11 = (bf16[256,1536]{1,0:T(8,128)(2,1)S(1)}, bf16[256,1536]{1,0:T(8,128)(2,1)}, u32[]{:S(2)}, u32[]{:S(2)}) collective-permute-start(bf16[256,1536]{1,0:T(8,128)(2,1)S(1)} %copy-done.23), channel_id=1, source_target_pairs={{0,64},{64,0},{1,65},{65,1},{2,66},{66,2},{3,67},{67,3},{4,68},{68... | collective-permute-start | bytes 2359304 | tf_op jit(solution)/shard_map/ppermute | solution.py:583
  26.2 7.8 %collective-permute-start.4 = (bf16[96,1920]{1,0:T(8,128)(2,1)S(1)}, bf16[96,1920]{1,0:T(8,128)(2,1)S(1)}, u32[]{:S(2)}, u32[]{:S(2)}) collective-permute-start(bf16[96,1920]{1,0:T(8,128)(2,1)S(1)} %pad_maximum_fusion.2), channel_id=1, source_target_pairs={{0,12},{1,13},{2,14},{3,15},{4,0},{5,1},{6,2},{7,3},{8,4},{9,5},{1... | collective-permute-start | bytes 1105928 | tf_op jit(solution)/shard_map/ppermute | solution.py:579
  27.9 8.7 %collective-permute-start.5 = (bf16[96,1920]{1,0:T(8,128)(2,1)S(1)}, bf16[96,1920]{1,0:T(8,128)(2,1)S(1)}, u32[]{:S(2)}, u32[]{:S(2)}) collective-permute-start(bf16[96,1920]{1,0:T(8,128)(2,1)S(1)} %pad_maximum_fusion.2), channel_id=1, source_target_pairs={{0,8},{1,9},{2,10},{3,11},{4,12},{5,13},{6,14},{7,15},{8,0},{9,1},... | collective-permute-start | bytes 1105928 | tf_op jit(solution)/shard_map/ppermute | solution.py:579
  30.0 10.9 %collective-permute-start.6 = (bf16[96,1920]{1,0:T(8,128)(2,1)S(1)}, bf16[96,1920]{1,0:T(8,128)(2,1)S(1)}, u32[]{:S(2)}, u32[]{:S(2)}) collective-permute-start(bf16[96,1920]{1,0:T(8,128)(2,1)S(1)} %pad_maximum_fusion.2), channel_id=1, source_target_pairs={{0,4},{1,5},{2,6},{3,7},{4,8},{5,9},{6,10},{7,11},{8,12},{9,13},{1... | collective-permute-start | bytes 1105928 | tf_op jit(solution)/shard_map/ppermute | solution.py:579
  41.7 41.2 %collective-permute-start.7 = (bf16[384,1920]{1,0:T(8,128)(2,1)}, bf16[384,1920]{1,0:T(8,128)(2,1)S(1)}, u32[]{:S(2)}, u32[]{:S(2)}) collective-permute-start(bf16[384,1920]{1,0:T(8,128)(2,1)} %constant_dynamic-update-slice_fusion.refs_0_), channel_id=1, source_target_pairs={{0,3},{1,0},{2,1},{3,2},{4,7},{5,4},{6,5},{7,6},{8,11},{9,8},{10,9... | collective-permute-start | bytes 4423688 | tf_op jit(solution)/shard_map/ppermute | solution.py:579
  44.4 39.7 %collective-permute-start.8 = (bf16[384,1920]{1,0:T(8,128)(2,1)}, bf16[384,1920]{1,0:T(8,128)(2,1)S(1)}, u32[]{:S(2)}, u32[]{:S(2)}) collective-permute-start(bf16[384,1920]{1,0:T(8,128)(2,1)} %constant_dynamic-update-slice_fusion.refs_0_), channel_id=1, source_target_pairs={{0,2},{1,3},{2,0},{3,1},{4,6},{5,7},{6,4},{7,5},{8,10},{9,11},{10,... | collective-permute-start | bytes 4423688 | tf_op jit(solution)/shard_map/ppermute | solution.py:579
  44.6 42.0 %collective-permute-start.9 = (bf16[384,1920]{1,0:T(8,128)(2,1)}, bf16[384,1920]{1,0:T(8,128)(2,1)S(1)}, u32[]{:S(2)}, u32[]{:S(2)}) collective-permute-start(bf16[384,1920]{1,0:T(8,128)(2,1)} %constant_dynamic-update-slice_fusion.refs_0_), channel_id=1, source_target_pairs={{0,1},{1,2},{2,3},{3,0},{4,5},{5,6},{6,7},{7,4},{8,9},{9,10},{10,1... | collective-permute-start | bytes 4423688 | tf_op jit(solution)/shard_map/ppermute | solution.py:579
  49.9 36.8 %copy-start.3 = (bf16[512,1536]{1,0:T(8,128)(2,1)}, bf16[512,1536]{1,0:T(8,128)(2,1)S(1)}, u32[]{:S(2)}) copy-start(bf16[512,1536]{1,0:T(8,128)(2,1)S(1)} %fusion.6.left_ref) | copy-start | bytes 4718596
  129.6 4.3 %collective-permute-start.12 = (bf16[512,1536]{1,0:T(8,128)(2,1)S(1)}, bf16[512,1536]{1,0:T(8,128)(2,1)S(1)}, u32[]{:S(2)}, u32[]{:S(2)}) collective-permute-start(bf16[512,1536]{1,0:T(8,128)(2,1)S(1)} %constant_dynamic-slice_fusion.1), channel_id=1, source_target_pairs={{0,64},{64,0},{1,65},{65,1},{2,66},{66,2},{3,67},{67,3},{4,68},{68... | collective-permute-start | bytes 4718600 | tf_op jit(solution)/shard_map/ppermute | solution.py:583
  137.5 1.3 collective-permute-start.13
  143.0 9.8 %copy-start.6 = (bf16[512,1536]{1,0:T(8,128)(2,1)}, bf16[512,1536]{1,0:T(8,128)(2,1)S(1)}, u32[]{:S(2)}) copy-start(bf16[512,1536]{1,0:T(8,128)(2,1)S(1)} %get-tuple-element.138.dgate_ref) | copy-start | bytes 4718596
  143.0 9.8 %copy-start.7 = (bf16[512,1536]{1,0:T(8,128)(2,1)}, bf16[512,1536]{1,0:T(8,128)(2,1)S(1)}, u32[]{:S(2)}) copy-start(bf16[512,1536]{1,0:T(8,128)(2,1)S(1)} %get-tuple-element.142.own_ref.own_mixed_ref) | copy-start | bytes 4718596
  143.0 3.4 %collective-permute-start.14 = (bf16[512,1536]{1,0:T(8,128)(2,1)S(1)}, bf16[512,1536]{1,0:T(8,128)(2,1)S(1)}, u32[]{:S(2)}, u32[]{:S(2)}) collective-permute-start(bf16[512,1536]{1,0:T(8,128)(2,1)S(1)} %get-tuple-element.142.own_ref.own_mixed_ref), channel_id=1, source_target_pairs={{0,64},{64,0},{1,65},{65,1},{2,66},{66,2},{3,67},{67,3},{4,68},{68... | collective-permute-start | bytes 4718600 | tf_op jit(solution)/shard_map/ppermute | solution.py:583
  160.9 19.0 %copy-start.4 = (bf16[512,1536]{1,0:T(8,128)(2,1)S(1)}, bf16[512,1536]{1,0:T(8,128)(2,1)}, u32[]{:S(2)}) copy-start(bf16[512,1536]{1,0:T(8,128)(2,1)} %copy-done.3) | copy-start | bytes 4718596
  185.8 30.5 %collective-permute-start.15 = (bf16[400,1920]{1,0:T(8,128)(2,1)}, bf16[400,1920]{1,0:T(8,128)(2,1)S(1)}, u32[]{:S(2)}, u32[]{:S(2)}) collective-permute-start(bf16[400,1920]{1,0:T(8,128)(2,1)} %get-tuple-element.95), channel_id=1, source_target_pairs={{0,1},{1,2},{2,3},{3,0},{4,5},{5,6},{6,7},{7,4},{8,9},{9,10},{10,1... | collective-permute-start | bytes 4608008 | tf_op jit(solution)/shard_map/ppermute | solution.py:579
  187.0 56.4 %collective-permute-start.16 = (bf16[400,1920]{1,0:T(8,128)(2,1)}, bf16[400,1920]{1,0:T(8,128)(2,1)S(1)}, u32[]{:S(2)}, u32[]{:S(2)}) collective-permute-start(bf16[400,1920]{1,0:T(8,128)(2,1)} %get-tuple-element.96), channel_id=1, source_target_pairs={{0,2},{1,3},{2,0},{3,1},{4,6},{5,7},{6,4},{7,5},{8,10},{9,11},{10,... | collective-permute-start | bytes 4608008 | tf_op jit(solution)/shard_map/ppermute | solution.py:579
  189.5 54.0 %collective-permute-start.17 = (bf16[400,1920]{1,0:T(8,128)(2,1)}, bf16[400,1920]{1,0:T(8,128)(2,1)S(1)}, u32[]{:S(2)}, u32[]{:S(2)}) collective-permute-start(bf16[400,1920]{1,0:T(8,128)(2,1)} %get-tuple-element.97), channel_id=1, source_target_pairs={{0,3},{1,0},{2,1},{3,2},{4,7},{5,4},{6,5},{7,6},{8,11},{9,8},{10,9... | collective-permute-start | bytes 4608008 | tf_op jit(solution)/shard_map/ppermute | solution.py:579
  247.6 3.8 %collective-permute-start.19 = (bf16[256,1536]{1,0:T(8,128)(2,1)}, bf16[256,1536]{1,0:T(8,128)(2,1)S(1)}, u32[]{:S(2)}, u32[]{:S(2)}) collective-permute-start(bf16[256,1536]{1,0:T(8,128)(2,1)} %get-tuple-element.119), channel_id=1, source_target_pairs={{0,64},{64,0},{1,65},{65,1},{2,66},{66,2},{3,67},{67,3},{4,68},{68... | collective-permute-start | bytes 2359304 | tf_op jit(solution)/shard_map/ppermute | solution.py:583
  247.6 10.0 %collective-permute-start.18 = (bf16[256,768]{1,0:T(8,128)(2,1)}, bf16[256,768]{1,0:T(8,128)(2,1)S(1)}, u32[]{:S(2)}, u32[]{:S(2)}) collective-permute-start(bf16[256,768]{1,0:T(8,128)(2,1)} %get-tuple-element.117), channel_id=1, source_target_pairs={{0,64},{64,0},{1,65},{65,1},{2,66},{66,2},{3,67},{67,3},{4,68},{68... | collective-permute-start | bytes 1179656 | tf_op jit(solution)/shard_map/ppermute | solution.py:583
  248.1 10.0 %copy-start.29 = (bf16[256,768]{1,0:T(8,128)(2,1)S(1)}, bf16[256,768]{1,0:T(8,128)(2,1)}, u32[]{:S(2)}) copy-start(bf16[256,768]{1,0:T(8,128)(2,1)} %get-tuple-element.116) | copy-start | bytes 1179652
  248.1 21.9 %collective-permute-start.20 = (bf16[112,1920]{1,0:T(8,128)(2,1)}, bf16[112,1920]{1,0:T(8,128)(2,1)S(1)}, u32[]{:S(2)}, u32[]{:S(2)}) collective-permute-start(bf16[112,1920]{1,0:T(8,128)(2,1)} %copy-done.16), channel_id=1, source_target_pairs={{0,4},{1,5},{2,6},{3,7},{4,8},{5,9},{6,10},{7,11},{8,12},{9,13},{1... | collective-permute-start | bytes 1290248 | tf_op jit(solution)/shard_map/ppermute | solution.py:579
  249.0 20.9 %collective-permute-start.21 = (bf16[112,1920]{1,0:T(8,128)(2,1)}, bf16[112,1920]{1,0:T(8,128)(2,1)S(1)}, u32[]{:S(2)}, u32[]{:S(2)}) collective-permute-start(bf16[112,1920]{1,0:T(8,128)(2,1)} %copy-done.15), channel_id=1, source_target_pairs={{0,8},{1,9},{2,10},{3,11},{4,12},{5,13},{6,14},{7,15},{8,0},{9,1},... | collective-permute-start | bytes 1290248 | tf_op jit(solution)/shard_map/ppermute | solution.py:579
  254.6 20.4 %copy-start.10 = (f32[112,1920]{1,0:T(8,128)S(1)}, f32[112,1920]{1,0:T(8,128)}, u32[]{:S(2)}) copy-start(f32[112,1920]{1,0:T(8,128)} %copy-done.9) | copy-start | bytes 2580484
  254.6 4.4 %collective-permute-start.23 = (f32[1,1536]{1,0:T(1,128)S(1)}, f32[1,1536]{1,0:T(1,128)S(1)}, u32[]{:S(2)}, u32[]{:S(2)}) collective-permute-start(f32[1,1536]{1,0:T(1,128)S(1)} %broadcast_in_dim.40), channel_id=1, source_target_pairs={{0,1},{1,2},{2,3},{3,0},{4,5},{5,6},{6,7},{7,4},{8,9},{9,10},{10,1... | collective-permute-start | bytes 18440 | tf_op jit(solution)/shard_map/ppermute | solution.py:579
  254.9 4.3 %collective-permute-start.24 = (f32[1,1536]{1,0:T(1,128)S(1)}, f32[1,1536]{1,0:T(1,128)S(1)}, u32[]{:S(2)}, u32[]{:S(2)}) collective-permute-start(f32[1,1536]{1,0:T(1,128)S(1)} %broadcast_in_dim.40), channel_id=1, source_target_pairs={{0,2},{1,3},{2,0},{3,1},{4,6},{5,7},{6,4},{7,5},{8,10},{9,11},{10,... | collective-permute-start | bytes 18440 | tf_op jit(solution)/shard_map/ppermute | solution.py:579
  257.6 3.0 collective-permute-start.25
  260.6 4.3 %collective-permute-start.26 = (f32[1,1536]{1,0:T(1,128)S(1)}, f32[1,1536]{1,0:T(1,128)S(1)}, u32[]{:S(2)}, u32[]{:S(2)}) collective-permute-start(f32[1,1536]{1,0:T(1,128)S(1)} %add_add_fusion.3), channel_id=1, source_target_pairs={{0,4},{1,5},{2,6},{3,7},{4,8},{5,9},{6,10},{7,11},{8,12},{9,13},{1... | collective-permute-start | bytes 18440 | tf_op jit(solution)/shard_map/ppermute | solution.py:579
  260.7 8.8 %collective-permute-start.27 = (f32[1,1536]{1,0:T(1,128)S(1)}, f32[1,1536]{1,0:T(1,128)S(1)}, u32[]{:S(2)}, u32[]{:S(2)}) collective-permute-start(f32[1,1536]{1,0:T(1,128)S(1)} %add_add_fusion.3), channel_id=1, source_target_pairs={{0,8},{1,9},{2,10},{3,11},{4,12},{5,13},{6,14},{7,15},{8,0},{9,1},... | collective-permute-start | bytes 18440 | tf_op jit(solution)/shard_map/ppermute | solution.py:579
  262.8 6.7 %collective-permute-start.28 = (f32[1,1536]{1,0:T(1,128)S(1)}, f32[1,1536]{1,0:T(1,128)S(1)}, u32[]{:S(2)}, u32[]{:S(2)}) collective-permute-start(f32[1,1536]{1,0:T(1,128)S(1)} %add_add_fusion.3), channel_id=1, source_target_pairs={{0,12},{1,13},{2,14},{3,15},{4,0},{5,1},{6,2},{7,3},{8,4},{9,5},{1... | collective-permute-start | bytes 18440 | tf_op jit(solution)/shard_map/ppermute | solution.py:579
  264.9 10.0 %collective-permute-start.22 = (bf16[112,1920]{1,0:T(8,128)(2,1)S(1)}, bf16[112,1920]{1,0:T(8,128)(2,1)S(1)}, u32[]{:S(2)}, u32[]{:S(2)}) collective-permute-start(bf16[112,1920]{1,0:T(8,128)(2,1)S(1)} %get-tuple-element.123), channel_id=1, source_target_pairs={{0,12},{1,13},{2,14},{3,15},{4,0},{5,1},{6,2},{7,3},{8,4},{9,5},{1... | collective-permute-start | bytes 1290248 | tf_op jit(solution)/shard_map/ppermute | solution.py:579
  277.1 9.8 %collective-permute-start.33 = (bf16[96,768]{1,0:T(8,128)(2,1)S(1)}, bf16[96,768]{1,0:T(8,128)(2,1)S(1)}, u32[]{:S(2)}, u32[]{:S(2)}) collective-permute-start(bf16[96,768]{1,0:T(8,128)(2,1)S(1)} %get-tuple-element.153), channel_id=1, source_target_pairs={{0,1},{1,2},{2,3},{3,0},{4,5},{5,6},{6,7},{7,4},{8,9},{9,10},{10,1... | collective-permute-start | bytes 442376 | tf_op jit(solution)/shard_map/ppermute | solution.py:781
  278.4 10.4 %collective-permute-start.34 = (bf16[96,768]{1,0:T(8,128)(2,1)S(1)}, bf16[96,768]{1,0:T(8,128)(2,1)S(1)}, u32[]{:S(2)}, u32[]{:S(2)}) collective-permute-start(bf16[96,768]{1,0:T(8,128)(2,1)S(1)} %get-tuple-element.155), channel_id=1, source_target_pairs={{0,2},{1,3},{2,0},{3,1},{4,6},{5,7},{6,4},{7,5},{8,10},{9,11},{10,... | collective-permute-start | bytes 442376 | tf_op jit(solution)/shard_map/ppermute | solution.py:781
  281.1 7.7 %collective-permute-start.35 = (bf16[96,768]{1,0:T(8,128)(2,1)S(1)}, bf16[96,768]{1,0:T(8,128)(2,1)S(1)}, u32[]{:S(2)}, u32[]{:S(2)}) collective-permute-start(bf16[96,768]{1,0:T(8,128)(2,1)S(1)} %get-tuple-element.154), channel_id=1, source_target_pairs={{0,3},{1,0},{2,1},{3,2},{4,7},{5,4},{6,5},{7,6},{8,11},{9,8},{10,9... | collective-permute-start | bytes 442376 | tf_op jit(solution)/shard_map/ppermute | solution.py:781
  285.8 7.9 %collective-permute-start.29 = (bf16[48,1920]{1,0:T(8,128)(2,1)S(1)}, bf16[48,1920]{1,0:T(8,128)(2,1)S(1)}, u32[]{:S(2)}, u32[]{:S(2)}) collective-permute-start(bf16[48,1920]{1,0:T(8,128)(2,1)S(1)} %get-tuple-element.129), channel_id=1, source_target_pairs={{0,16},{1,17},{2,18},{3,19},{4,20},{5,21},{6,22},{7,23},{8,24},{9,... | collective-permute-start | bytes 552968 | tf_op jit(solution)/shard_map/ppermute | solution.py:579
  286.4 7.3 %collective-permute-start.30 = (bf16[48,1920]{1,0:T(8,128)(2,1)S(1)}, bf16[48,1920]{1,0:T(8,128)(2,1)S(1)}, u32[]{:S(2)}, u32[]{:S(2)}) collective-permute-start(bf16[48,1920]{1,0:T(8,128)(2,1)S(1)} %get-tuple-element.130), channel_id=1, source_target_pairs={{0,32},{1,33},{2,34},{3,35},{4,36},{5,37},{6,38},{7,39},{8,40},{9,... | collective-permute-start | bytes 552968 | tf_op jit(solution)/shard_map/ppermute | solution.py:579
  287.0 7.0 %collective-permute-start.31 = (bf16[48,1920]{1,0:T(8,128)(2,1)S(1)}, bf16[48,1920]{1,0:T(8,128)(2,1)S(1)}, u32[]{:S(2)}, u32[]{:S(2)}) collective-permute-start(bf16[48,1920]{1,0:T(8,128)(2,1)S(1)} %get-tuple-element.131), channel_id=1, source_target_pairs={{0,48},{1,49},{2,50},{3,51},{4,52},{5,53},{6,54},{7,55},{8,56},{9,... | collective-permute-start | bytes 552968 | tf_op jit(solution)/shard_map/ppermute | solution.py:579
  288.8 13.5 %collective-permute-start.36 = (f32[96,768]{1,0:T(8,128)S(1)}, f32[96,768]{1,0:T(8,128)S(1)}, u32[]{:S(2)}, u32[]{:S(2)}) collective-permute-start(f32[96,768]{1,0:T(8,128)S(1)} %convert_add_fusion.3), channel_id=1, source_target_pairs={{0,64},{64,0},{1,65},{65,1},{2,66},{66,2},{3,67},{67,3},{4,68},{68... | collective-permute-start | bytes 884744 | tf_op jit(solution)/shard_map/ppermute | solution.py:583
  294.1 4.3 %collective-permute-start.32 = (f32[8,1920]{1,0:T(8,128)S(1)}, f32[8,1920]{1,0:T(8,128)S(1)}, u32[]{:S(2)}, u32[]{:S(2)}) collective-permute-start(f32[8,1920]{1,0:T(8,128)S(1)} %slice_add_fusion), channel_id=1, source_target_pairs={{0,64},{64,0},{1,65},{65,1},{2,66},{66,2},{3,67},{67,3},{4,68},{68... | collective-permute-start | bytes 184328 | tf_op jit(solution)/shard_map/ppermute | solution.py:583
  297.6 4.7 %collective-permute-start.37 = (f32[24,1920]{1,0:T(8,128)S(1)}, f32[24,1920]{1,0:T(8,128)S(1)}, u32[]{:S(2)}, u32[]{:S(2)}) collective-permute-start(f32[24,1920]{1,0:T(8,128)S(1)} %slice.292), channel_id=1, source_target_pairs={{0,64},{64,0},{1,65},{65,1},{2,66},{66,2},{3,67},{67,3},{4,68},{68... | collective-permute-start | bytes 552968 | tf_op jit(solution)/shard_map/ppermute | solution.py:583
  (37 other events, 169.9 us)
Sparse Core Ops, SparseCore 0:
  11.4 111.3 all-gather.1
  156.6 116.0 reduce-scatter.1
